TPU v7x, 32 devices: a whole 2x2x4 slice. The times are simulated.
32 devices in a mesh: groups: 2 (over x), seq: 16 (over z, y, core).
Axes of the slice: x: 2, y: 2, z: 4, core: 2. Of those that a mesh axis runs over, the one named last changes fastest.
Arguments:
- queries: bfloat16 [256, 2560], P(('groups', 'seq')), parts along dimension 0, may hold values from -130 to 130
- cache_keys: bfloat16 [32768, 2560], P(('groups', 'seq')), parts along dimension 0, may hold values from -6 to 6
- cache_values: bfloat16 [32768, 2560], P(('groups', 'seq')), parts along dimension 0, may hold values from -6 to 6
- span_keys: bfloat16 [256, 2560], P(('groups', 'seq')), parts along dimension 0, may hold values from -8 to 8
- span_values: bfloat16 [256, 2560], P(('groups', 'seq')), parts along dimension 0, may hold values from -6 to 6
- cache_tokens: int32 [2], P('groups'), parts along dimension 0, may hold values from 8192 to 16384
- span_start: int32 [2], P('groups'), parts along dimension 0, may hold values from 1433 to 1559
Outputs:
- attended: bfloat16 [256, 2560], P(('groups', 'seq')), parts along dimension 0
There are 2 independent parts, one for each index of `groups`. A program takes and returns all parts, laid end to end along the dimension named above; each array names one. Nothing has to cross between parts.
All inputs are finite; a program needn't handle non-finite values.
Results may differ from a plain program's by a relative error of at most 0.0026.
Values may be sent and summed in bfloat16 or wider, within the bound.
A program may use at most 320 MiB of HBM per device.

v0:
```python
import math

import jax
import jax.numpy as jnp
from jax import lax
from jax.sharding import PartitionSpec as P

HEAD_DIM = 128
HEADS = 20
FRAME_TOK = 1560


NEG_FILL = -1e30


def local(queries, cache_keys, cache_values, span_keys, span_values, cache_tokens, span_start):
    device_index = lax.axis_index("seq")
    cache_rows = cache_keys.shape[0]
    own_tokens = queries.shape[0]
    score_scale = 1.0 / math.sqrt(HEAD_DIM)
    valid_end = cache_tokens[0]
    frame_offset = span_start[0]
    all_queries = lax.all_gather(queries, "seq", axis=0, tiled=True)
    total_rows = all_queries.shape[0]
    query_heads = all_queries.reshape(total_rows, HEADS, HEAD_DIM)
    slot_ids = jnp.arange(cache_rows, dtype=jnp.int32)
    key_rows, value_rows = (cache_keys, cache_values)
    position = device_index * cache_rows + slot_ids
    used_rows = jnp.clip(valid_end - device_index * cache_rows, 0, cache_rows)
    key_rows = key_rows.reshape(cache_rows, HEADS, HEAD_DIM)
    value_rows = value_rows.reshape(cache_rows, HEADS, HEAD_DIM)
    block_rows = min(512, cache_rows)
    block_total = cache_rows // block_rows
    block_count = (used_rows + block_rows - 1) // block_rows
    query_frame = (frame_offset + jnp.arange(total_rows, dtype=jnp.int32)) // FRAME_TOK
    key_frame = (
        frame_offset + device_index * own_tokens + jnp.arange(own_tokens, dtype=jnp.int32)
    ) // FRAME_TOK
    own_keys = span_keys.reshape(own_tokens, HEADS, HEAD_DIM)
    own_values = span_values.reshape(own_tokens, HEADS, HEAD_DIM)
    span_scores = (
        jnp.einsum("qhd,khd->hqk", query_heads, own_keys, preferred_element_type=jnp.float32)
        * score_scale
    )
    span_scores = jnp.where(
        (key_frame[None, :] <= query_frame[:, None])[None], span_scores, NEG_FILL
    )

    def block_scores(step_index):
        begin = step_index * block_rows
        key_piece = lax.dynamic_slice_in_dim(key_rows, begin, block_rows, 0)
        scores = (
            jnp.einsum("qhd,khd->hqk", query_heads, key_piece, preferred_element_type=jnp.float32)
            * score_scale
        )
        spot = lax.dynamic_slice_in_dim(position, begin, block_rows, 0)
        return jnp.where((spot < valid_end)[None, None, :], scores, NEG_FILL)

    def store_step(step_index, stored):
        return lax.dynamic_update_index_in_dim(stored, block_scores(step_index), step_index, 0)

    empty_store = jnp.full((block_total, HEADS, total_rows, block_rows), NEG_FILL, jnp.float32)
    stored = lax.fori_loop(0, block_count, store_step, empty_store)
    local_top = jnp.maximum(jnp.max(span_scores, axis=2), jnp.max(stored, axis=(0, 3)))
    row_top = lax.pmax(local_top, "seq")

    def weigh(scores, value_piece):
        weights = jnp.exp(scores - row_top[:, :, None])
        rounded = weights.astype(jnp.bfloat16)
        numer = jnp.einsum("hqk,khd->qhd", rounded, value_piece, preferred_element_type=jnp.float32)
        return (jnp.sum(weights, axis=2), numer)

    first_den, first_num = weigh(span_scores, own_values)

    def sum_step(step_index, running):
        value_piece = lax.dynamic_slice_in_dim(value_rows, step_index * block_rows, block_rows, 0)
        scores = lax.dynamic_index_in_dim(stored, step_index, 0, keepdims=False)
        part_den, part_num = weigh(scores, value_piece)
        return (running[0] + part_den, running[1] + part_num)

    denominator, numerator = lax.fori_loop(0, block_count, sum_step, (first_den, first_num))
    numerator = numerator.reshape(total_rows, HEADS * HEAD_DIM)
    mine_num, mine_den = (
        lax.psum_scatter(numerator, "seq", scatter_dimension=0, tiled=True),
        lax.psum_scatter(denominator, "seq", scatter_dimension=1, tiled=True),
    )
    attended = mine_num.reshape(own_tokens, HEADS, HEAD_DIM) / jnp.transpose(mine_den)[:, :, None]
    return attended.reshape(own_tokens, HEADS * HEAD_DIM).astype(jnp.bfloat16)


def solution(mesh):
    placed = (
        P(("groups", "seq"), None),
        P(("groups", "seq"), None),
        P(("groups", "seq"), None),
        P(("groups", "seq"), None),
        P(("groups", "seq"), None),
        P("groups"),
        P("groups"),
    )
    return jax.shard_map(
        local, mesh=mesh, in_specs=placed, out_specs=P(("groups", "seq"), None), check_vma=False
    )
```

profile of v0, /device:TPU:0, one launch (start us, length us, event | category | flops | bytes accessed | tf_op | source)
XLA Modules:
  0.0 235.5 jit_solution(13375473434348146988)
XLA Ops:
  6.5 0.0 copy-start
  6.5 0.0 reduce-scatter.5.cloned.1.call-start
  7.2 25.3 %all_gather.3 = bf16[128,2560]{1,0:T(8,128)(2,1)S(1)} all-gather(bf16[8,2560]{1,0:T(8,128)(2,1)} %param.11), channel_id=1, replica_groups=mesh['groups'=2,'seq'=16] {'seq'}, dimensions={0}, use_global_device_ids=true | all-gather | bytes 696320 | tf_op jit(solution)/shard_map/all_gather | solution.py:23
  32.6 0.3 copy.21
  32.9 0.4 copy.25
  33.3 8.0 %copy.23 = bf16[1024,2560]{0,1:T(8,128)(2,1)} copy(bf16[1024,2560]{1,0:T(8,128)(2,1)} %param.12) | data formatting | bytes 10485760 | tf_op args[1]
  41.2 5.2 %broadcast_in_dim.40 = f32[2,20,128,512]{2,3,1,0:T(8,128)} broadcast(f32[]{:T(128)} %constant.76.clone.1), dimensions={} | broadcast | bytes 10485764 | tf_op jit(solution)/shard_map/broadcast_in_dim | solution.py:62
  46.5 12.3 %while.22 = (s32[]{:T(128)}, f32[2,20,128,512]{2,3,1,0:T(8,128)}, s32[]{:T(128)}, s32[1024]{0:T(1024)S(1)}, s32[]{:T(128)}, /*index=5*/bf16[1024,20,128]{0,2,1:T...) while((s32[]{:T(128)}, f32[2,20,128,512]{2,3,1,0:T(8,128)}, ...), condition=%wide.region_2.3_spmd, body=%wide.region_1.2_spmd.sunk | while | flops 338166272 | bytes 8522965 | solution.py:63
  46.5 0.7 dynamic-slice_compare_fusion.2
  47.2 5.4 %bitcast_dynamic-update-slice_fusion.2 = f32[2,20,128,512]{2,3,1,0:T(8,128)} fusion(f32[2,20,128,512]{2,3,1,0:T(8,128)} %get-tuple-element.251, s32[]{:T(128)S(6)} %select_n.63, pred[512]{0:T(512)(128)(4,1)S(1)} %dynamic-slice_compare_fusion.2, bf16[128,20,128]{2,0,1:T(8,128)(2,1)S(1)} %get-tuple-element.268, ...), kind=kOutput, calls=%fused_computation.clone.1 | convolution fusion | flops 338165760 | bytes 8520200 | tf_op jit(solution)/shard_map/while/body/qhd,khd->hqk/dot_general | solution.py:53
  52.6 0.7 dynamic-slice_compare_fusion.2
  53.3 5.4 %bitcast_dynamic-update-slice_fusion.2 = f32[2,20,128,512]{2,3,1,0:T(8,128)} fusion(f32[2,20,128,512]{2,3,1,0:T(8,128)} %get-tuple-element.251, s32[]{:T(128)S(6)} %select_n.63, pred[512]{0:T(512)(128)(4,1)S(1)} %dynamic-slice_compare_fusion.2, bf16[128,20,128]{2,0,1:T(8,128)(2,1)S(1)} %get-tuple-element.268, ...), kind=kOutput, calls=%fused_computation.clone.1 | convolution fusion | flops 338165760 | bytes 8520200 | tf_op jit(solution)/shard_map/while/body/qhd,khd->hqk/dot_general | solution.py:53
  59.5 0.0 copy-start.2
  59.5 4.5 %reduce_max.19 = f32[20,128]{1,0:T(8,128)S(1)} reduce(f32[2,20,128,512]{2,3,1,0:T(8,128)} %get-tuple-element.278, f32[]{:T(128)} %constant.77.clone.1), dimensions={0,3}, to_apply=%region_3.4 | reduce | flops 2618880 | bytes 10496004 | tf_op jit(solution)/shard_map/reduce_max | solution.py:64
  63.9 0.1 broadcast_compare_fusion
  64.0 0.0 copy-done.2
  64.0 0.3 fusion.31
  64.3 57.8 %pmax.7 = f32[20,128]{1,0:T(8,128)S(1)} all-reduce(f32[20,128]{1,0:T(8,128)S(1)} %max.10), channel_id=1, replica_groups=mesh['groups'=2,'seq'=16] {'seq'}, use_global_device_ids=true, to_apply=%region_4.5 | all-reduce | flops 2560 | bytes 20480 | tf_op jit(solution)/shard_map/pmax | solution.py:65
  122.2 0.0 copy-done
  122.2 0.4 convolution_bitcast_fusion
  122.6 0.4 copy.27
  123.0 8.0 %copy.26 = bf16[1024,2560]{0,1:T(8,128)(2,1)} copy(bf16[1024,2560]{1,0:T(8,128)(2,1)} %param.13) | data formatting | bytes 10485760 | tf_op args[2]
  131.0 0.0 copy-start.3
  131.0 34.7 %while.23 = (s32[]{:T(128)}, f32[20,128]{1,0:T(8,128)S(1)}, f32[128,20,128]{0,2,1:T(8,128)S(1)}, s32[]{:T(128)}, f32[2,20,128,512]{2,3,1,0:T(8,128)}, /*index=5*...) while((s32[]{:T(128)}, f32[20,128]{1,0:T(8,128)S(1)}, ...), condition=%wide.region_8.9_spmd, body=%wide.region_6.8_spmd.sunk | while | flops 341114880 | bytes 57733352 | solution.py:81
  131.0 5.2 %constant_dynamic-slice_fusion.2 = f32[1,20,128,512]{2,3,1,0:T(8,128)} fusion(f32[2,20,128,512]{2,3,1,0:T(8,128)} %get-tuple-element.302, s32[]{:T(128)S(6)} %select_n.65), kind=kLoop, calls=%fused_computation.15.clone.1 | loop fusion | bytes 10485764 | tf_op jit(solution)/shard_map/while/body/jit(dynamic_index_in_dim)/dynamic_slice | solution.py:77
  136.2 6.0 %copy.38 = f32[1,20,128,512]{3,2,1,0:T(8,128)} copy(f32[1,20,128,512]{2,3,1,0:T(8,128)} %constant_dynamic-slice_fusion.2) | data formatting | bytes 10485760 | tf_op jit(solution)/shard_map/while/body/jit(dynamic_index_in_dim)/dynamic_slice | solution.py:77
  142.2 0.0 copy-start.1
  142.2 4.7 %fusion.45 = f32[128,20,128]{0,2,1:T(8,128)S(1)} fusion(f32[128,20,128]{0,2,1:T(8,128)S(1)} %get-tuple-element.288, f32[1,20,128,512]{3,2,1,0:T(8,128)} %copy.38, f32[20,128]{1,0:T(8,128)S(1)} %get-tuple-element.303, bf16[1024,20,128]{0,2,1:T(8,128)(2,1)} %get-tuple-element.304, s32[]{:T(128)S(6)} %select_n.66), kind=kOutput, calls=%fused_computation.13.clone.1 | convolution fusion | flops 338493440 | bytes 10496004 | tf_op jit(solution)/shard_map/while/body/hqk,khd->qhd/dot_general | solution.py:70
  146.9 0.1 copy-done.1
  147.0 1.4 fusion.44
  148.4 5.2 %constant_dynamic-slice_fusion.2 = f32[1,20,128,512]{2,3,1,0:T(8,128)} fusion(f32[2,20,128,512]{2,3,1,0:T(8,128)} %get-tuple-element.302, s32[]{:T(128)S(6)} %select_n.65), kind=kLoop, calls=%fused_computation.15.clone.1 | loop fusion | bytes 10485764 | tf_op jit(solution)/shard_map/while/body/jit(dynamic_index_in_dim)/dynamic_slice | solution.py:77
  153.6 6.0 %copy.38 = f32[1,20,128,512]{3,2,1,0:T(8,128)} copy(f32[1,20,128,512]{2,3,1,0:T(8,128)} %constant_dynamic-slice_fusion.2) | data formatting | bytes 10485760 | tf_op jit(solution)/shard_map/while/body/jit(dynamic_index_in_dim)/dynamic_slice | solution.py:77
  159.6 0.0 copy-start.1
  159.6 4.7 %fusion.45 = f32[128,20,128]{0,2,1:T(8,128)S(1)} fusion(f32[128,20,128]{0,2,1:T(8,128)S(1)} %get-tuple-element.288, f32[1,20,128,512]{3,2,1,0:T(8,128)} %copy.38, f32[20,128]{1,0:T(8,128)S(1)} %get-tuple-element.303, bf16[1024,20,128]{0,2,1:T(8,128)(2,1)} %get-tuple-element.304, s32[]{:T(128)S(6)} %select_n.66), kind=kOutput, calls=%fused_computation.13.clone.1 | convolution fusion | flops 338493440 | bytes 10496004 | tf_op jit(solution)/shard_map/while/body/hqk,khd->qhd/dot_general | solution.py:70
  164.3 0.0 copy-done.1
  164.3 1.4 fusion.44
  165.7 1.5 copy.31
  167.2 0.0 reduce-scatter.5.cloned.1.call-update
  167.2 0.0 copy-done.3
  167.2 0.6 dynamic-slice
  168.4 57.9 %all-reduce = f32[20,128]{1,0:T(8,128)S(1)} all-reduce(f32[20,128]{1,0:T(8,128)S(1)} %get-tuple-element.84), channel_id=3, replica_groups=mesh['groups'=2,'seq'=16] {'seq'}, use_global_device_ids=true, to_apply=%region_10.11.clone | all-reduce | flops 2560 | bytes 20480
  226.3 0.1 dynamic-slice_bitcast_fusion
  226.4 0.0 reduce-scatter.5.cloned.1.call-done
  226.4 1.3 copy.32
  227.7 0.1 fusion.23
  227.8 0.9 copy.29
  (7 shorter events, 0.1 us)
Async XLA Ops:
  6.5 115.7 %copy-start = (bf16[8,2560]{1,0:T(8,128)(2,1)S(1)}, bf16[8,2560]{1,0:T(8,128)(2,1)}, u32[]{:S(2)}) copy-start(bf16[8,2560]{1,0:T(8,128)(2,1)} %param.15) | copy-start | bytes 122884
  6.5 219.8 %reduce-scatter.5.cloned.1.call-start = ((), (), s32[]{:S(2)}) async-start(), calls=%async_computation.1 | async-start | bytes 1392640
  59.5 4.6 %copy-start.2 = (bf16[8,2560]{1,0:T(8,128)(2,1)S(1)}, bf16[8,2560]{1,0:T(8,128)(2,1)}, u32[]{:S(2)}) copy-start(bf16[8,2560]{1,0:T(8,128)(2,1)} %param.14) | copy-start | bytes 122884
  131.0 36.2 %copy-start.3 = (u32[32]{0:T(128)S(1)}, u32[32]{0:T(128)}, u32[]{:S(2)}) copy-start(u32[32]{0:T(128)} %constant.89) | copy-start | bytes 388
  142.2 4.8 %copy-start.1 = (f32[1,20,128,512]{3,2,1,0:T(8,128)S(1)}, f32[1,20,128,512]{3,2,1,0:T(8,128)}, u32[]{:S(2)}) copy-start(f32[1,20,128,512]{3,2,1,0:T(8,128)} %copy.38) | copy-start | bytes 15728644 | tf_op jit(solution)/shard_map/while
  159.6 4.8 %copy-start.1 = (f32[1,20,128,512]{3,2,1,0:T(8,128)S(1)}, f32[1,20,128,512]{3,2,1,0:T(8,128)}, u32[]{:S(2)}) copy-start(f32[1,20,128,512]{3,2,1,0:T(8,128)} %copy.38) | copy-start | bytes 15728644 | tf_op jit(solution)/shard_map/while
Sparse Core Ops, SparseCore 0:
  167.3 55.8 reduce-scatter.4
where the time goes:
time: 236 us
  blocking collectives  141 us (60%)
  local copies, waits for them, and re-layouts  49 us (21%)
  matrix products  21 us (9%)
  between operations  15.5 us (7%)
  other arithmetic  8.89 us (4%)
    unnamed x1, blocking collectives  57.9 us
    pmax x1, blocking collectives, local(): row_top = lax.pmax(local_top, 'seq')  57.8 us
    all_gather x1, blocking collectives, local(): all_queries = lax.all_gather(queries, 'seq', axis=0, tiled=True)  25.3 us
    dynamic_slice x4, local copies, waits for them, and re-layouts, sum_step(): scores = lax.dynamic_index_in_dim(stored, step_index, 0, keepdims=False)  22.4 us
    unnamed x11, local copies, waits for them, and re-layouts  19.3 us
    dot_general x2, matrix products, block_scores(): jnp.einsum('qhd,khd->hqk', query_heads, key_piece, preferred_element_type...  10.9 us
    dot_general x3, matrix products, weigh(): jnp.einsum('hqk,khd->qhd', rounded, value_piece, preferred_element_type=j...  9.82 us
    broadcast_in_dim x1, local copies, waits for them, and re-layouts, local(): jnp.full((block_total, HEADS, total_rows, block_rows), NEG_FILL, jnp.floa...  5.23 us
  transfers between devices with their start and end apart: 1, of which 0 were waited for; matrix products, arithmetic and copies ran while one was open for 0% of the time, Pallas kernels for 0%

commit v1 on v0

v1 whole, which is shorter than its diff:
```python
import functools
import math

import jax
import jax.numpy as jnp
from jax import lax
from jax.experimental import pallas as pl
from jax.experimental.pallas import tpu as pltpu
from jax.sharding import PartitionSpec as P

HEAD_DIM = 128
FRAME_TOK = 1560
NEG_FILL = -1e30
LANES = 128
MESH = pl.DeviceIdType.MESH


def merge(x, y, heads):
    width = heads * HEAD_DIM
    sx, sy = x[:, width:], y[:, width:]
    top = jnp.maximum(sx, sy)
    fx, fy = jnp.exp2(sx - top), jnp.exp2(sy - top)
    lane = lax.broadcasted_iota(jnp.int32, sx.shape, 1)
    den = sx * pltpu.roll(fx, 64, 1) + sy * pltpu.roll(fy, 64, 1)
    pieces = []
    for j in range(heads):
        cut = slice(j * HEAD_DIM, (j + 1) * HEAD_DIM)
        pieces.append(x[:, cut] * fx[:, j : j + 1] + y[:, cut] * fy[:, j : j + 1])
    pieces.append(jnp.where(lane < 64, top, den))
    return jnp.concatenate(pieces, axis=1)


def kernel(
    n, chunks,
    tok_ref, start_ref, q_ref, k_hbm, v_hbm, sk_ref, sv_ref, o_ref,
    qg, kbuf, vbuf, part, ra, rb, rc, bias_row, bias_span,
    kv_sem, g_send, g_recv, a_send, a_recv, b_send, b_recv, c_send, c_recv,
):
    rows, width = k_hbm.shape
    own = q_ref.shape[0]
    chips = n // 2
    far = chips // 2
    total = n * own
    heads = width // HEAD_DIM // chunks
    cw = heads * HEAD_DIM
    cs = cw + LANES
    coef = math.log2(math.e) / math.sqrt(HEAD_DIM)

    me = lax.axis_index("seq")
    group = lax.axis_index("groups")
    core = lax.rem(me, 2)
    side = lax.rem(me // 2, 2)
    hi = me // 4

    def device(hi_, side_, core_):
        return (group, (hi_ * 2 + side_) * 2 + core_)

    def slot_of(hi_, side_, core_):
        return core_ * chips + side_ * far + hi_

    sibling = device(hi, side, 1 - core)
    across = device(hi, 1 - side, core)

    def kv_copy(c, which):
        cut = pl.ds(pl.multiple_of(c * cw, LANES), cw)
        src, dst = (k_hbm, kbuf) if which == 0 else (v_hbm, vbuf)
        return pltpu.make_async_copy(
            src.at[:, cut], dst.at[pl.ds(0, rows), cut], kv_sem.at[which, c]
        )

    for c in range(chunks):
        kv_copy(c, 0).start()
        kv_copy(c, 1).start()

    barrier = pltpu.get_barrier_semaphore()
    pl.semaphore_signal(barrier, inc=1, device_id=sibling, device_id_type=MESH)
    pl.semaphore_signal(barrier, inc=1, device_id=across, device_id_type=MESH)
    for d in range(1, far):
        pl.semaphore_signal(
            barrier, inc=1, device_id=device(lax.rem(hi + d, far), side, core), device_id_type=MESH
        )

    my_slot = slot_of(hi, side, core)
    qg[pl.ds(my_slot, 1)] = q_ref[...][None]

    pl.semaphore_wait(barrier, far + 1)

    def gather_copy(slot, to, number):
        return pltpu.make_async_remote_copy(
            src_ref=qg.at[slot], dst_ref=qg.at[slot],
            send_sem=g_send.at[number], recv_sem=g_recv.at[slot],
            device_id=to, device_id_type=MESH,
        )

    sends = []

    def gather_send(slot, to):
        copy = gather_copy(slot, to, len(sends))
        copy.start()
        sends.append(copy)

    def gather_wait(slot):
        gather_copy(slot, sibling, 0).wait_recv()

    for d in range(1, far):
        gather_send(my_slot, device(lax.rem(hi + d, far), side, core))
    gather_send(my_slot, across)
    gather_send(my_slot, sibling)

    position = me * rows + lax.broadcasted_iota(jnp.int32, bias_row.shape, 1)
    bias_row[...] = jnp.where(position < tok_ref[0], 0.0, NEG_FILL)
    shape = (total, LANES)
    row = lax.broadcasted_iota(jnp.int32, shape, 0)
    lane = lax.broadcasted_iota(jnp.int32, shape, 1)
    token = row
    for s in range(n):
        s_core, s_side, s_hi = s // chips, (s % chips) // far, s % far
        owner = (s_hi * 2 + s_side) * 2 + s_core
        inside = jnp.logical_and(row >= s * own, row < (s + 1) * own)
        token = jnp.where(inside, row + (owner - s) * own, token)
    key = me * own + lane
    seen = lane < own
    for f in range(1, (FRAME_TOK - 1 + total) // FRAME_TOK + 1):
        edge = f * FRAME_TOK - start_ref[0]
        seen = jnp.logical_and(seen, jnp.logical_or(key < edge, token >= edge))
    bias_span[...] = jnp.where(seen, 0.0, NEG_FILL)
    pad = jnp.zeros((LANES - own, width), jnp.float32)
    for ref, buf in ((sk_ref, kbuf), (sv_ref, vbuf)):
        block = jnp.concatenate([ref[...].astype(jnp.float32), pad], axis=0)
        buf[pl.ds(rows, LANES), :] = block.astype(jnp.bfloat16)

    for d in range(1, far):
        slot = slot_of(lax.rem(hi - d + far, far), side, core)
        gather_wait(slot)
        gather_send(slot, across)
        gather_send(slot, sibling)
    for d in range(far):
        slot = slot_of(lax.rem(hi - d + far, far), 1 - side, core)
        gather_wait(slot)
        gather_send(slot, sibling)
    for s_side in (side, 1 - side):
        for d in range(far):
            gather_wait(slot_of(lax.rem(hi - d + far, far), s_side, 1 - core))

    def a_copy(c):
        return pltpu.make_async_remote_copy(
            src_ref=part.at[c, pl.ds((1 - core) * chips, chips)], dst_ref=ra.at[c],
            send_sem=a_send.at[c], recv_sem=a_recv.at[c],
            device_id=sibling, device_id_type=MESH,
        )

    def b_copy(c):
        return pltpu.make_async_remote_copy(
            src_ref=part.at[c, pl.ds(core * chips + (1 - side) * far, far)], dst_ref=rb.at[c],
            send_sem=b_send.at[c], recv_sem=b_recv.at[c],
            device_id=across, device_id_type=MESH,
        )

    def c_copy(c, d):
        other = lax.rem(hi + d, far)
        return pltpu.make_async_remote_copy(
            src_ref=part.at[c, slot_of(other, side, core)], dst_ref=rc.at[c, d - 1],
            send_sem=c_send.at[c, d - 1], recv_sem=c_recv.at[c, d - 1],
            device_id=device(other, side, core), device_id_type=MESH,
        )

    def attend(c):
        kv_copy(c, 0).wait()
        kv_copy(c, 1).wait()
        stat_lane = lax.broadcasted_iota(jnp.int32, (total, LANES), 1)
        stats = jnp.zeros((total, LANES), jnp.float32)
        for j in range(heads):
            cut = pl.ds(pl.multiple_of(c * cw + j * HEAD_DIM, LANES), HEAD_DIM)
            q = qg[:, :, cut].astype(jnp.float32).reshape(total, HEAD_DIM).astype(jnp.bfloat16)
            s = lax.dot_general(
                q, kbuf[:, cut], (((1,), (1,)), ((), ())), preferred_element_type=jnp.float32
            ) * coef
            s_cache = s[:, :rows] + bias_row[...]
            s_span = s[:, rows:] + bias_span[...]
            s = jnp.concatenate([s_cache, s_span], axis=1)
            top = jnp.max(s, axis=1, keepdims=True)
            w = jnp.exp2(s - top)
            den = jnp.sum(w, axis=1, keepdims=True)
            high = w.astype(jnp.bfloat16)
            low = (w - high.astype(jnp.float32)).astype(jnp.bfloat16)
            both = jnp.dot(
                jnp.concatenate([high, low], axis=0), vbuf[:, cut],
                preferred_element_type=jnp.float32,
            )
            num = both[:total] + both[total:]
            part[c, :, :, j * HEAD_DIM : (j + 1) * HEAD_DIM] = num.reshape(n, own, HEAD_DIM)
            stats = jnp.where(stat_lane == j, top, stats)
            stats = jnp.where(stat_lane == 64 + j, den, stats)
        part[c, :, :, cw:] = stats.reshape(n, own, LANES)

    def merge_a(c):
        a_copy(c).wait_recv()
        mine = pl.ds(core * chips, chips)
        x = part[c, mine].reshape(chips * own, cs)
        y = ra[c].reshape(chips * own, cs)
        part[c, mine] = merge(x, y, heads).reshape(chips, own, cs)
        b_copy(c).start()

    def merge_b(c):
        b_copy(c).wait_recv()
        mine = pl.ds(core * chips + side * far, far)
        x = part[c, mine].reshape(far * own, cs)
        y = rb[c].reshape(far * own, cs)
        part[c, mine] = merge(x, y, heads).reshape(far, own, cs)
        for d in range(1, far):
            c_copy(c, d).start()

    def finish(c):
        x = part[c, my_slot]
        for d in range(1, far):
            c_copy(c, d).wait_recv()
            x = merge(x, rc[c, d - 1], heads)
        out = [
            x[:, j * HEAD_DIM : (j + 1) * HEAD_DIM] / x[:, cw + 64 + j : cw + 65 + j]
            for j in range(heads)
        ]
        cut = pl.ds(pl.multiple_of(c * cw, LANES), cw)
        o_ref[:, cut] = jnp.concatenate(out, axis=1).astype(jnp.bfloat16)

    def step(t, _):
        @pl.when(t < chunks)
        def _():
            attend(t)
            a_copy(t).start()

        @pl.when(jnp.logical_and(t >= 1, t < chunks + 1))
        def _():
            merge_a(t - 1)

        @pl.when(jnp.logical_and(t >= 2, t < chunks + 2))
        def _():
            merge_b(t - 2)

        @pl.when(t >= 3)
        def _():
            finish(t - 3)

        return 0

    lax.fori_loop(0, chunks + 3, step, 0)

    for copy in sends:
        copy.wait_send()
    for c in range(chunks):
        a_copy(c).wait_send()
        b_copy(c).wait_send()
        for d in range(1, far):
            c_copy(c, d).wait_send()


def local(n, queries, cache_keys, cache_values, span_keys, span_values, cache_tokens, span_start):
    own, width = queries.shape
    rows = cache_keys.shape[0]
    heads = width // HEAD_DIM
    chunks = 4 if heads % 4 == 0 else 1
    chips = n // 2
    far = chips // 2
    total = n * own
    cs = width // chunks + LANES
    smem = pl.BlockSpec(memory_space=pltpu.SMEM)
    vmem = pl.BlockSpec(memory_space=pltpu.VMEM)
    hbm = pl.BlockSpec(memory_space=pl.ANY)
    dma = pltpu.SemaphoreType.DMA
    return pl.pallas_call(
        functools.partial(kernel, n, chunks),
        out_shape=jax.ShapeDtypeStruct((own, width), jnp.bfloat16),
        in_specs=[smem, smem, vmem, hbm, hbm, vmem, vmem],
        out_specs=vmem,
        scratch_shapes=[
            pltpu.VMEM((n, own, width), jnp.bfloat16),
            pltpu.VMEM((rows + LANES, width), jnp.bfloat16),
            pltpu.VMEM((rows + LANES, width), jnp.bfloat16),
            pltpu.VMEM((chunks, n, own, cs), jnp.float32),
            pltpu.VMEM((chunks, chips, own, cs), jnp.float32),
            pltpu.VMEM((chunks, far, own, cs), jnp.float32),
            pltpu.VMEM((chunks, far - 1, own, cs), jnp.float32),
            pltpu.VMEM((1, rows), jnp.float32),
            pltpu.VMEM((total, LANES), jnp.float32),
            dma((2, chunks)),
            dma((far - 1 + far + chips,)),
            dma((n,)),
            dma((chunks,)),
            dma((chunks,)),
            dma((chunks,)),
            dma((chunks,)),
            dma((chunks, far - 1)),
            dma((chunks, far - 1)),
        ],
        compiler_params=pltpu.CompilerParams(
            collective_id=0, has_side_effects=True, vmem_limit_bytes=56 * 1024 * 1024
        ),
    )(cache_tokens, span_start, queries, cache_keys, cache_values, span_keys, span_values)


def solution(mesh):
    placed = (
        P(("groups", "seq"), None),
        P(("groups", "seq"), None),
        P(("groups", "seq"), None),
        P(("groups", "seq"), None),
        P(("groups", "seq"), None),
        P("groups"),
        P("groups"),
    )
    return jax.shard_map(
        functools.partial(local, mesh.shape["seq"]),
        mesh=mesh, in_specs=placed, out_specs=P(("groups", "seq"), None), check_vma=False,
    )
```

time: 236 us -> 42.3 us (0.18)
  blocking collectives: 141 us -> 0 us
  local copies, waits for them, and re-layouts: 49 us -> 1.4 us
  Pallas kernels: 0 us -> 39.4 us
  matrix products: 21 us -> 0 us
  between operations: 15.5 us -> 1.3 us
  other arithmetic: 8.89 us -> 0 us
    unnamed x1 -> x0, blocking collectives: 57.9 us -> none
    pmax x1 -> x0, blocking collectives: 57.8 us -> none  [local(): row_top = lax.pmax(local_top, 'seq')]
    pallas_call x0 -> x1, Pallas kernels: none -> 39.4 us  [local(): pl.pallas_call(functools.partial(kernel, n, chunks), out_shape=jax.ShapeD...]
    all_gather x1 -> x0, blocking collectives: 25.3 us -> none  [local(): all_queries = lax.all_gather(queries, 'seq', axis=0, tiled=True)]
    dynamic_slice x4 -> x0, local copies, waits for them, and re-layouts: 22.4 us -> none  [sum_step(): scores = lax.dynamic_index_in_dim(stored, step_index, 0, keepdims=False)]
    dot_general x6 -> x0, matrix products: 21 us -> none  [the longest x2 10.9 us: block_scores(): jnp.einsum('qhd,khd->hqk', query_heads, key_piece, preferred_element_type...]
    unnamed x11 -> x1, local copies, waits for them, and re-layouts: 19.3 us -> 1.4 us
    broadcast_in_dim x1 -> x0, local copies, waits for them, and re-layouts: 5.23 us -> none  [local(): jnp.full((block_total, HEADS, total_rows, block_rows), NEG_FILL, jnp.floa...]
  transfers between devices with their start and end apart: 1 -> 0, of which waited for: 0 -> 0; matrix products, arithmetic and copies ran while one was open for 0% -> 0% of each run, Pallas kernels for 0% -> 0%
where the time goes in v1:
time: 42.3 us; the launch traced here: 42.1 us
  Pallas kernels  39.4 us (93%)
  local copies, waits for them, and re-layouts  1.4 us (3%)
  between operations  1.3 us (3%)
    pallas_call x1, Pallas kernels, local(): pl.pallas_call(functools.partial(kernel, n, chunks), out_shape=jax.ShapeD...  39.4 us
    unnamed x1, local copies, waits for them, and re-layouts  1.4 us

profile of v1, /device:TPU:0, one launch (start us, length us, event | category | flops | bytes accessed | tf_op | source)
XLA Modules:
  0.0 42.1 jit_solution(16742292523302889301)
XLA Ops:
  1.3 39.4 %shard_map.73 = bf16[8,2560]{1,0:T(8,128)(2,1)} custom-call(s32[1]{0:T(128)S(6)} %copy.9.tok_ref, s32[1]{0:T(128)S(6)} %copy.10.start_ref, bf16[8,2560]{1,0:T(8,128)(2,1)} %q_ref.1, bf16[1024,2560]{1,0:T(8,128)(2,1)} %k_hbm.1, bf16[1024,2560]{1,0:T(8,128)(2,1)} %v_hbm.1, bf16[8,2560]{1,0:T(8,128)(2,1)} %sk_ref.1, bf16[8,2560]{1,0:T(8,128)(2,1)} %sv_ref.1), custom_call_target="tpu_custom_call" | custom-call | tf_op jit(solution)/shard_map/pallas_call | solution.py:269
  40.7 1.4 %copy.11 = bf16[8,2560]{1,0:T(8,128)(2,1)} copy(bf16[8,2560]{1,0:T(8,128)(2,1)} %shard_map.73) | data formatting | bytes 81920

commit v2 on v1

--- a/solution.py
+++ b/solution.py
@@ -81,31 +81,49 @@
         )
 
     my_slot = slot_of(hi, side, core)
-    qg[pl.ds(my_slot, 1)] = q_ref[...][None]
+    for c in range(chunks):
+        qg[c, pl.ds(my_slot, 1)] = q_ref[:, c * cw : (c + 1) * cw][None]
 
     pl.semaphore_wait(barrier, far + 1)
 
-    def gather_copy(slot, to, number):
+    def gather_copy(c, slot, to, number):
         return pltpu.make_async_remote_copy(
-            src_ref=qg.at[slot], dst_ref=qg.at[slot],
-            send_sem=g_send.at[number], recv_sem=g_recv.at[slot],
+            src_ref=qg.at[c, slot], dst_ref=qg.at[c, slot],
+            send_sem=g_send.at[c, number], recv_sem=g_recv.at[c, slot],
             device_id=to, device_id_type=MESH,
         )
 
-    sends = []
-
-    def gather_send(slot, to):
-        copy = gather_copy(slot, to, len(sends))
-        copy.start()
-        sends.append(copy)
-
-    def gather_wait(slot):
-        gather_copy(slot, sibling, 0).wait_recv()
-
-    for d in range(1, far):
-        gather_send(my_slot, device(lax.rem(hi + d, far), side, core))
-    gather_send(my_slot, across)
-    gather_send(my_slot, sibling)
+    def from_behind(d):
+        return lax.rem(hi - d + far, far)
+
+    def gather_own(c):
+        for d in range(1, far):
+            to = device(lax.rem(hi + d, far), side, core)
+            gather_copy(c, my_slot, to, d - 1).start()
+        gather_copy(c, my_slot, across, far - 1).start()
+        gather_copy(c, my_slot, sibling, 2 * far - 1).start()
+
+    def gather_far(c):
+        for d in range(1, far):
+            slot = slot_of(from_behind(d), side, core)
+            gather_copy(c, slot, sibling, 0).wait_recv()
+            gather_copy(c, slot, across, far - 1 + d).start()
+            gather_copy(c, slot, sibling, 2 * far - 1 + d).start()
+
+    def gather_across(c):
+        for d in range(far):
+            slot = slot_of(from_behind(d), 1 - side, core)
+            gather_copy(c, slot, sibling, 0).wait_recv()
+            gather_copy(c, slot, sibling, 3 * far - 1 + d).start()
+
+    def gather_sibling(c):
+        for s_side in (side, 1 - side):
+            for d in range(far):
+                slot = slot_of(from_behind(d), s_side, 1 - core)
+                gather_copy(c, slot, sibling, 0).wait_recv()
+
+    for c in range(chunks):
+        gather_own(c)
 
     position = me * rows + lax.broadcasted_iota(jnp.int32, bias_row.shape, 1)
     bias_row[...] = jnp.where(position < tok_ref[0], 0.0, NEG_FILL)
@@ -123,24 +141,19 @@
     for f in range(1, (FRAME_TOK - 1 + total) // FRAME_TOK + 1):
         edge = f * FRAME_TOK - start_ref[0]
         seen = jnp.logical_and(seen, jnp.logical_or(key < edge, token >= edge))
-    bias_span[...] = jnp.where(seen, 0.0, NEG_FILL)
+    seen_bias = jnp.where(seen, 0.0, NEG_FILL)
+    bias_span[pl.ds(0, total)] = seen_bias
+    bias_span[pl.ds(total, total)] = seen_bias
     pad = jnp.zeros((LANES - own, width), jnp.float32)
     for ref, buf in ((sk_ref, kbuf), (sv_ref, vbuf)):
         block = jnp.concatenate([ref[...].astype(jnp.float32), pad], axis=0)
         buf[pl.ds(rows, LANES), :] = block.astype(jnp.bfloat16)
 
-    for d in range(1, far):
-        slot = slot_of(lax.rem(hi - d + far, far), side, core)
-        gather_wait(slot)
-        gather_send(slot, across)
-        gather_send(slot, sibling)
-    for d in range(far):
-        slot = slot_of(lax.rem(hi - d + far, far), 1 - side, core)
-        gather_wait(slot)
-        gather_send(slot, sibling)
-    for s_side in (side, 1 - side):
-        for d in range(far):
-            gather_wait(slot_of(lax.rem(hi - d + far, far), s_side, 1 - core))
+    gather_far(0)
+    gather_across(0)
+    if chunks > 1:
+        gather_far(1)
+    gather_sibling(0)
 
     def a_copy(c):
         return pltpu.make_async_remote_copy(
@@ -164,34 +177,33 @@
             device_id=device(other, side, core), device_id_type=MESH,
         )
 
-    def attend(c):
-        kv_copy(c, 0).wait()
-        kv_copy(c, 1).wait()
+    def attend(c, pair, stats):
+        begin = pair * 2 * HEAD_DIM
+        cut = pl.ds(pl.multiple_of(c * cw + begin, LANES), 2 * HEAD_DIM)
+        q = qg[c, :, :, begin : begin + 2 * HEAD_DIM].astype(jnp.float32)
+        q = q.reshape(total, 2 * HEAD_DIM)
+        first = lax.broadcasted_iota(jnp.int32, q.shape, 1) < HEAD_DIM
+        q = jnp.concatenate([jnp.where(first, q, 0.0), jnp.where(first, 0.0, q)], axis=0)
+        s = lax.dot_general(
+            q.astype(jnp.bfloat16), kbuf[:, cut], (((1,), (1,)), ((), ())),
+            preferred_element_type=jnp.float32,
+        ) * coef
+        s_cache = s[:, :rows] + bias_row[...]
+        s_span = s[:, rows:] + bias_span[...]
+        s = jnp.concatenate([s_cache, s_span], axis=1)
+        top = jnp.max(s, axis=1, keepdims=True)
+        w = jnp.exp2(s - top)
+        den = jnp.sum(w, axis=1, keepdims=True)
+        num = jnp.dot(w.astype(jnp.bfloat16), vbuf[:, cut], preferred_element_type=jnp.float32)
         stat_lane = lax.broadcasted_iota(jnp.int32, (total, LANES), 1)
-        stats = jnp.zeros((total, LANES), jnp.float32)
-        for j in range(heads):
-            cut = pl.ds(pl.multiple_of(c * cw + j * HEAD_DIM, LANES), HEAD_DIM)
-            q = qg[:, :, cut].astype(jnp.float32).reshape(total, HEAD_DIM).astype(jnp.bfloat16)
-            s = lax.dot_general(
-                q, kbuf[:, cut], (((1,), (1,)), ((), ())), preferred_element_type=jnp.float32
-            ) * coef
-            s_cache = s[:, :rows] + bias_row[...]
-            s_span = s[:, rows:] + bias_span[...]
-            s = jnp.concatenate([s_cache, s_span], axis=1)
-            top = jnp.max(s, axis=1, keepdims=True)
-            w = jnp.exp2(s - top)
-            den = jnp.sum(w, axis=1, keepdims=True)
-            high = w.astype(jnp.bfloat16)
-            low = (w - high.astype(jnp.float32)).astype(jnp.bfloat16)
-            both = jnp.dot(
-                jnp.concatenate([high, low], axis=0), vbuf[:, cut],
-                preferred_element_type=jnp.float32,
-            )
-            num = both[:total] + both[total:]
-            part[c, :, :, j * HEAD_DIM : (j + 1) * HEAD_DIM] = num.reshape(n, own, HEAD_DIM)
-            stats = jnp.where(stat_lane == j, top, stats)
-            stats = jnp.where(stat_lane == 64 + j, den, stats)
+        for i in range(2):
+            j, own_rows = 2 * pair + i, slice(i * total, (i + 1) * total)
+            piece = num[own_rows, i * HEAD_DIM : (i + 1) * HEAD_DIM]
+            part[c, :, :, j * HEAD_DIM : (j + 1) * HEAD_DIM] = piece.reshape(n, own, HEAD_DIM)
+            stats = jnp.where(stat_lane == j, top[own_rows], stats)
+            stats = jnp.where(stat_lane == 64 + j, den[own_rows], stats)
         part[c, :, :, cw:] = stats.reshape(n, own, LANES)
+        return stats
 
     def merge_a(c):
         a_copy(c).wait_recv()
@@ -222,31 +234,38 @@
         cut = pl.ds(pl.multiple_of(c * cw, LANES), cw)
         o_ref[:, cut] = jnp.concatenate(out, axis=1).astype(jnp.bfloat16)
 
+    def when(low, t, high, do, c):
+        @pl.when(jnp.logical_and(t >= low, t < high))
+        def _():
+            do(c)
+
+    def open_chunk(c):
+        kv_copy(c, 0).wait()
+        kv_copy(c, 1).wait()
+        attend(c, 0, jnp.zeros((total, LANES), jnp.float32))
+
+    def close_chunk(c):
+        stats = part[c, :, :, cw:].reshape(total, LANES)
+        for pair in range(1, heads // 2):
+            stats = attend(c, pair, stats)
+        a_copy(c).start()
+
     def step(t, _):
-        @pl.when(t < chunks)
-        def _():
-            attend(t)
-            a_copy(t).start()
-
-        @pl.when(jnp.logical_and(t >= 1, t < chunks + 1))
-        def _():
-            merge_a(t - 1)
-
-        @pl.when(jnp.logical_and(t >= 2, t < chunks + 2))
-        def _():
-            merge_b(t - 2)
-
-        @pl.when(t >= 3)
-        def _():
-            finish(t - 3)
-
+        when(1, t, chunks, gather_sibling, t)
+        when(0, t, chunks, open_chunk, t)
+        when(0, t, chunks - 2, gather_far, t + 2)
+        when(0, t, chunks - 1, gather_across, t + 1)
+        when(1, t, chunks + 1, merge_a, t - 1)
+        when(2, t, chunks + 2, merge_b, t - 2)
+        when(3, t, chunks + 3, finish, t - 3)
+        when(0, t, chunks, close_chunk, t)
         return 0
 
     lax.fori_loop(0, chunks + 3, step, 0)
 
-    for copy in sends:
-        copy.wait_send()
     for c in range(chunks):
+        for number in range(2 * far - 1 + chips):
+            gather_copy(c, my_slot, sibling, number).wait_send()
         a_copy(c).wait_send()
         b_copy(c).wait_send()
         for d in range(1, far):
@@ -257,7 +276,7 @@
     own, width = queries.shape
     rows = cache_keys.shape[0]
     heads = width // HEAD_DIM
-    chunks = 4 if heads % 4 == 0 else 1
+    chunks = heads // (4 if heads % 4 == 0 else 2)
     chips = n // 2
     far = chips // 2
     total = n * own
@@ -272,7 +291,7 @@
         in_specs=[smem, smem, vmem, hbm, hbm, vmem, vmem],
         out_specs=vmem,
         scratch_shapes=[
-            pltpu.VMEM((n, own, width), jnp.bfloat16),
+            pltpu.VMEM((chunks, n, own, width // chunks), jnp.bfloat16),
             pltpu.VMEM((rows + LANES, width), jnp.bfloat16),
             pltpu.VMEM((rows + LANES, width), jnp.bfloat16),
             pltpu.VMEM((chunks, n, own, cs), jnp.float32),
@@ -280,10 +299,10 @@
             pltpu.VMEM((chunks, far, own, cs), jnp.float32),
             pltpu.VMEM((chunks, far - 1, own, cs), jnp.float32),
             pltpu.VMEM((1, rows), jnp.float32),
-            pltpu.VMEM((total, LANES), jnp.float32),
+            pltpu.VMEM((2 * total, LANES), jnp.float32),
             dma((2, chunks)),
-            dma((far - 1 + far + chips,)),
-            dma((n,)),
+            dma((chunks, far - 1 + far + chips)),
+            dma((chunks, n)),
             dma((chunks,)),
             dma((chunks,)),
             dma((chunks,)),

time: 42.3 us -> 45.3 us (1.071)
  Pallas kernels: 39.4 us -> 42.4 us
    pallas_call x1, Pallas kernels: 39.4 us -> 42.4 us  [local(): pl.pallas_call(functools.partial(kernel, n, chunks), out_shape=jax.ShapeD...]
where the time goes in v2:
time: 45.3 us; the launch traced here: 45.1 us
  Pallas kernels  42.4 us (94%)
  local copies, waits for them, and re-layouts  1.4 us (3%)
  between operations  1.3 us (3%)
    pallas_call x1, Pallas kernels, local(): pl.pallas_call(functools.partial(kernel, n, chunks), out_shape=jax.ShapeD...  42.4 us
    unnamed x1, local copies, waits for them, and re-layouts  1.4 us

profile of v2, /device:TPU:0, one launch (start us, length us, event | category | flops | bytes accessed | tf_op | source)
XLA Modules:
  0.0 45.1 jit_solution(17847566187840784837)
XLA Ops:
  1.3 42.4 %shard_map.73 = bf16[8,2560]{1,0:T(8,128)(2,1)} custom-call(s32[1]{0:T(128)S(6)} %copy.9.tok_ref, s32[1]{0:T(128)S(6)} %copy.10.start_ref, bf16[8,2560]{1,0:T(8,128)(2,1)} %q_ref.1, bf16[1024,2560]{1,0:T(8,128)(2,1)} %k_hbm.1, bf16[1024,2560]{1,0:T(8,128)(2,1)} %v_hbm.1, bf16[8,2560]{1,0:T(8,128)(2,1)} %sk_ref.1, bf16[8,2560]{1,0:T(8,128)(2,1)} %sv_ref.1), custom_call_target="tpu_custom_call" | custom-call | tf_op jit(solution)/shard_map/pallas_call | solution.py:288
  43.7 1.4 %copy.11 = bf16[8,2560]{1,0:T(8,128)(2,1)} copy(bf16[8,2560]{1,0:T(8,128)(2,1)} %shard_map.73) | data formatting | bytes 81920

commit v3 on v1

--- a/solution.py
+++ b/solution.py
@@ -164,12 +164,13 @@
             device_id=device(other, side, core), device_id_type=MESH,
         )
 
-    def attend(c):
-        kv_copy(c, 0).wait()
-        kv_copy(c, 1).wait()
+    def attend(c, first, last):
         stat_lane = lax.broadcasted_iota(jnp.int32, (total, LANES), 1)
-        stats = jnp.zeros((total, LANES), jnp.float32)
-        for j in range(heads):
+        if first == 0:
+            stats = jnp.zeros((total, LANES), jnp.float32)
+        else:
+            stats = part[c, :, :, cw:].reshape(total, LANES)
+        for j in range(first, last):
             cut = pl.ds(pl.multiple_of(c * cw + j * HEAD_DIM, LANES), HEAD_DIM)
             q = qg[:, :, cut].astype(jnp.float32).reshape(total, HEAD_DIM).astype(jnp.bfloat16)
             s = lax.dot_general(
@@ -181,13 +182,7 @@
             top = jnp.max(s, axis=1, keepdims=True)
             w = jnp.exp2(s - top)
             den = jnp.sum(w, axis=1, keepdims=True)
-            high = w.astype(jnp.bfloat16)
-            low = (w - high.astype(jnp.float32)).astype(jnp.bfloat16)
-            both = jnp.dot(
-                jnp.concatenate([high, low], axis=0), vbuf[:, cut],
-                preferred_element_type=jnp.float32,
-            )
-            num = both[:total] + both[total:]
+            num = jnp.dot(w.astype(jnp.bfloat16), vbuf[:, cut], preferred_element_type=jnp.float32)
             part[c, :, :, j * HEAD_DIM : (j + 1) * HEAD_DIM] = num.reshape(n, own, HEAD_DIM)
             stats = jnp.where(stat_lane == j, top, stats)
             stats = jnp.where(stat_lane == 64 + j, den, stats)
@@ -222,24 +217,28 @@
         cut = pl.ds(pl.multiple_of(c * cw, LANES), cw)
         o_ref[:, cut] = jnp.concatenate(out, axis=1).astype(jnp.bfloat16)
 
+    def when(low, t, high, do, c):
+        @pl.when(jnp.logical_and(t >= low, t < high))
+        def _():
+            do(c)
+
+    half = heads // 2
+
+    def open_chunk(c):
+        kv_copy(c, 0).wait()
+        kv_copy(c, 1).wait()
+        attend(c, 0, half)
+
+    def close_chunk(c):
+        attend(c, half, heads)
+        a_copy(c).start()
+
     def step(t, _):
-        @pl.when(t < chunks)
-        def _():
-            attend(t)
-            a_copy(t).start()
-
-        @pl.when(jnp.logical_and(t >= 1, t < chunks + 1))
-        def _():
-            merge_a(t - 1)
-
-        @pl.when(jnp.logical_and(t >= 2, t < chunks + 2))
-        def _():
-            merge_b(t - 2)
-
-        @pl.when(t >= 3)
-        def _():
-            finish(t - 3)
-
+        when(0, t, chunks, open_chunk, t)
+        when(1, t, chunks + 1, merge_a, t - 1)
+        when(2, t, chunks + 2, merge_b, t - 2)
+        when(3, t, chunks + 3, finish, t - 3)
+        when(0, t, chunks, close_chunk, t)
         return 0
 
     lax.fori_loop(0, chunks + 3, step, 0)

time: 42.3 us -> 42.7 us (level)
  no operation moved by 1% of the time
where the time goes in v3:
time: 42.7 us; the launch traced here: 42.5 us
  Pallas kernels  39.8 us (93%)
  local copies, waits for them, and re-layouts  1.4 us (3%)
  between operations  1.3 us (3%)
    pallas_call x1, Pallas kernels, local(): pl.pallas_call(functools.partial(kernel, n, chunks), out_shape=jax.ShapeD...  39.8 us
    unnamed x1, local copies, waits for them, and re-layouts  1.4 us

profile of v3, /device:TPU:0, one launch (start us, length us, event | category | flops | bytes accessed | tf_op | source)
XLA Modules:
  0.0 42.5 jit_solution(13351699147697199758)
XLA Ops:
  1.3 39.8 %shard_map.73 = bf16[8,2560]{1,0:T(8,128)(2,1)} custom-call(s32[1]{0:T(128)S(6)} %copy.9.tok_ref, s32[1]{0:T(128)S(6)} %copy.10.start_ref, bf16[8,2560]{1,0:T(8,128)(2,1)} %q_ref.1, bf16[1024,2560]{1,0:T(8,128)(2,1)} %k_hbm.1, bf16[1024,2560]{1,0:T(8,128)(2,1)} %v_hbm.1, bf16[8,2560]{1,0:T(8,128)(2,1)} %sk_ref.1, bf16[8,2560]{1,0:T(8,128)(2,1)} %sv_ref.1), custom_call_target="tpu_custom_call" | custom-call | tf_op jit(solution)/shard_map/pallas_call | solution.py:268
  41.1 1.4 %copy.11 = bf16[8,2560]{1,0:T(8,128)(2,1)} copy(bf16[8,2560]{1,0:T(8,128)(2,1)} %shard_map.73) | data formatting | bytes 81920

commit v4 on v3

--- a/solution.py
+++ b/solution.py
@@ -10,9 +10,50 @@
 
 HEAD_DIM = 128
 FRAME_TOK = 1560
-NEG_FILL = -1e30
+NEG_FILL = -(2.0**100)
+SPREAD = 240.0
 LANES = 128
 MESH = pl.DeviceIdType.MESH
+
+
+def two_parts(x):
+    high = x.astype(jnp.bfloat16).astype(jnp.float32)
+    return high, (x - high).astype(jnp.bfloat16).astype(jnp.float32)
+
+
+def code(x, heads):
+    width = heads * HEAD_DIM
+    stats = x[:, width:]
+    high, low = two_parts(stats)
+    tile = high + pltpu.roll(low, 16, 1)
+    lane = lax.broadcasted_iota(jnp.int32, stats.shape, 1)
+    pieces = []
+    for j in range(heads):
+        v = x[:, j * HEAD_DIM : (j + 1) * HEAD_DIM]
+        size = jnp.abs(v)
+        largest = jnp.max(size, axis=1, keepdims=True)
+        largest = largest.astype(jnp.bfloat16).astype(jnp.float32)
+        y = jnp.exp2(size * (SPREAD / jnp.maximum(largest, 1e-30)) - SPREAD / 2)
+        pieces.append(jnp.where(v < 0.0, -y, y).astype(jnp.bfloat16))
+        tile = jnp.where(lane == 32 + j, largest, tile)
+    pieces.append(tile.astype(jnp.bfloat16))
+    return jnp.concatenate(pieces, axis=1)
+
+
+def decode(y, heads):
+    width = heads * HEAD_DIM
+    tile = y[:, width:].astype(jnp.float32)
+    lane = lax.broadcasted_iota(jnp.int32, tile.shape, 1)
+    kept = jnp.logical_or(lane < 16, jnp.logical_and(lane >= 64, lane < 80))
+    stats = jnp.where(kept, tile + pltpu.roll(tile, LANES - 16, 1), 0.0)
+    pieces = []
+    for j in range(heads):
+        v = y[:, j * HEAD_DIM : (j + 1) * HEAD_DIM].astype(jnp.float32)
+        size = jnp.log(jnp.abs(v)) * (1.0 / (SPREAD * math.log(2.0))) + 0.5
+        size = size * tile[:, 32 + j : 33 + j]
+        pieces.append(jnp.where(v < 0.0, -size, size))
+    pieces.append(stats)
+    return jnp.concatenate(pieces, axis=1)
 
 
 def merge(x, y, heads):
@@ -33,7 +74,7 @@
 def kernel(
     n, chunks,
     tok_ref, start_ref, q_ref, k_hbm, v_hbm, sk_ref, sv_ref, o_ref,
-    qg, kbuf, vbuf, part, ra, rb, rc, bias_row, bias_span,
+    qg, kbuf, vbuf, part, ea, eb, ec, ra, rb, rc, bias_row, bias_span,
     kv_sem, g_send, g_recv, a_send, a_recv, b_send, b_recv, c_send, c_recv,
 ):
     rows, width = k_hbm.shape
@@ -144,14 +185,14 @@
 
     def a_copy(c):
         return pltpu.make_async_remote_copy(
-            src_ref=part.at[c, pl.ds((1 - core) * chips, chips)], dst_ref=ra.at[c],
+            src_ref=ea.at[c], dst_ref=ra.at[c],
             send_sem=a_send.at[c], recv_sem=a_recv.at[c],
             device_id=sibling, device_id_type=MESH,
         )
 
     def b_copy(c):
         return pltpu.make_async_remote_copy(
-            src_ref=part.at[c, pl.ds(core * chips + (1 - side) * far, far)], dst_ref=rb.at[c],
+            src_ref=eb.at[c], dst_ref=rb.at[c],
             send_sem=b_send.at[c], recv_sem=b_recv.at[c],
             device_id=across, device_id_type=MESH,
         )
@@ -159,7 +200,7 @@
     def c_copy(c, d):
         other = lax.rem(hi + d, far)
         return pltpu.make_async_remote_copy(
-            src_ref=part.at[c, slot_of(other, side, core)], dst_ref=rc.at[c, d - 1],
+            src_ref=ec.at[c, d - 1], dst_ref=rc.at[c, d - 1],
             send_sem=c_send.at[c, d - 1], recv_sem=c_recv.at[c, d - 1],
             device_id=device(other, side, core), device_id_type=MESH,
         )
@@ -179,7 +220,8 @@
             s_cache = s[:, :rows] + bias_row[...]
             s_span = s[:, rows:] + bias_span[...]
             s = jnp.concatenate([s_cache, s_span], axis=1)
-            top = jnp.max(s, axis=1, keepdims=True)
+            high, low = two_parts(jnp.max(s, axis=1, keepdims=True))
+            top = high + low
             w = jnp.exp2(s - top)
             den = jnp.sum(w, axis=1, keepdims=True)
             num = jnp.dot(w.astype(jnp.bfloat16), vbuf[:, cut], preferred_element_type=jnp.float32)
@@ -192,24 +234,27 @@
         a_copy(c).wait_recv()
         mine = pl.ds(core * chips, chips)
         x = part[c, mine].reshape(chips * own, cs)
-        y = ra[c].reshape(chips * own, cs)
-        part[c, mine] = merge(x, y, heads).reshape(chips, own, cs)
+        x = merge(x, decode(ra[c], heads), heads)
+        part[c, mine] = x.reshape(chips, own, cs)
+        theirs = part[c, pl.ds(core * chips + (1 - side) * far, far)]
+        eb[c] = code(theirs.reshape(far * own, cs), heads)
         b_copy(c).start()
 
     def merge_b(c):
         b_copy(c).wait_recv()
         mine = pl.ds(core * chips + side * far, far)
         x = part[c, mine].reshape(far * own, cs)
-        y = rb[c].reshape(far * own, cs)
-        part[c, mine] = merge(x, y, heads).reshape(far, own, cs)
+        x = merge(x, decode(rb[c], heads), heads)
+        part[c, mine] = x.reshape(far, own, cs)
         for d in range(1, far):
+            ec[c, d - 1] = code(part[c, slot_of(lax.rem(hi + d, far), side, core)], heads)
             c_copy(c, d).start()
 
     def finish(c):
         x = part[c, my_slot]
         for d in range(1, far):
             c_copy(c, d).wait_recv()
-            x = merge(x, rc[c, d - 1], heads)
+            x = merge(x, decode(rc[c, d - 1], heads), heads)
         out = [
             x[:, j * HEAD_DIM : (j + 1) * HEAD_DIM] / x[:, cw + 64 + j : cw + 65 + j]
             for j in range(heads)
@@ -231,6 +276,8 @@
 
     def close_chunk(c):
         attend(c, half, heads)
+        theirs = part[c, pl.ds((1 - core) * chips, chips)]
+        ea[c] = code(theirs.reshape(chips * own, cs), heads)
         a_copy(c).start()
 
     def step(t, _):
@@ -275,9 +322,12 @@
             pltpu.VMEM((rows + LANES, width), jnp.bfloat16),
             pltpu.VMEM((rows + LANES, width), jnp.bfloat16),
             pltpu.VMEM((chunks, n, own, cs), jnp.float32),
-            pltpu.VMEM((chunks, chips, own, cs), jnp.float32),
-            pltpu.VMEM((chunks, far, own, cs), jnp.float32),
-            pltpu.VMEM((chunks, far - 1, own, cs), jnp.float32),
+            pltpu.VMEM((chunks, chips * own, cs), jnp.bfloat16),
+            pltpu.VMEM((chunks, far * own, cs), jnp.bfloat16),
+            pltpu.VMEM((chunks, far - 1, own, cs), jnp.bfloat16),
+            pltpu.VMEM((chunks, chips * own, cs), jnp.bfloat16),
+            pltpu.VMEM((chunks, far * own, cs), jnp.bfloat16),
+            pltpu.VMEM((chunks, far - 1, own, cs), jnp.bfloat16),
             pltpu.VMEM((1, rows), jnp.float32),
             pltpu.VMEM((total, LANES), jnp.float32),
             dma((2, chunks)),

time: 42.7 us -> 42.7 us (level)
  no operation moved by 1% of the time
where the time goes in v4:
time: 42.7 us; the launch traced here: 42.4 us
  Pallas kernels  39.7 us (93%)
  local copies, waits for them, and re-layouts  1.4 us (3%)
  between operations  1.3 us (3%)
    pallas_call x1, Pallas kernels, local(): pl.pallas_call(functools.partial(kernel, n, chunks), out_shape=jax.ShapeD...  39.7 us
    unnamed x1, local copies, waits for them, and re-layouts  1.4 us

profile of v4, /device:TPU:0, one launch (start us, length us, event | category | flops | bytes accessed | tf_op | source)
XLA Modules:
  0.0 42.4 jit_solution(16642501890105691854)
XLA Ops:
  1.3 39.7 %shard_map.73 = bf16[8,2560]{1,0:T(8,128)(2,1)} custom-call(s32[1]{0:T(128)S(6)} %copy.9.tok_ref, s32[1]{0:T(128)S(6)} %copy.10.start_ref, bf16[8,2560]{1,0:T(8,128)(2,1)} %q_ref.1, bf16[1024,2560]{1,0:T(8,128)(2,1)} %k_hbm.1, bf16[1024,2560]{1,0:T(8,128)(2,1)} %v_hbm.1, bf16[8,2560]{1,0:T(8,128)(2,1)} %sk_ref.1, bf16[8,2560]{1,0:T(8,128)(2,1)} %sv_ref.1), custom_call_target="tpu_custom_call" | custom-call | tf_op jit(solution)/shard_map/pallas_call | solution.py:315
  41.0 1.4 %copy.11 = bf16[8,2560]{1,0:T(8,128)(2,1)} copy(bf16[8,2560]{1,0:T(8,128)(2,1)} %shard_map.73) | data formatting | bytes 81920

commit v5 on v4

--- a/solution.py
+++ b/solution.py
@@ -71,22 +71,9 @@
     return jnp.concatenate(pieces, axis=1)
 
 
-def kernel(
-    n, chunks,
-    tok_ref, start_ref, q_ref, k_hbm, v_hbm, sk_ref, sv_ref, o_ref,
-    qg, kbuf, vbuf, part, ea, eb, ec, ra, rb, rc, bias_row, bias_span,
-    kv_sem, g_send, g_recv, a_send, a_recv, b_send, b_recv, c_send, c_recv,
-):
-    rows, width = k_hbm.shape
-    own = q_ref.shape[0]
+def gather_kernel(n, q_ref, qg, g_send, g_recv):
     chips = n // 2
     far = chips // 2
-    total = n * own
-    heads = width // HEAD_DIM // chunks
-    cw = heads * HEAD_DIM
-    cs = cw + LANES
-    coef = math.log2(math.e) / math.sqrt(HEAD_DIM)
-
     me = lax.axis_index("seq")
     group = lax.axis_index("groups")
     core = lax.rem(me, 2)
@@ -101,17 +88,6 @@
 
     sibling = device(hi, side, 1 - core)
     across = device(hi, 1 - side, core)
-
-    def kv_copy(c, which):
-        cut = pl.ds(pl.multiple_of(c * cw, LANES), cw)
-        src, dst = (k_hbm, kbuf) if which == 0 else (v_hbm, vbuf)
-        return pltpu.make_async_copy(
-            src.at[:, cut], dst.at[pl.ds(0, rows), cut], kv_sem.at[which, c]
-        )
-
-    for c in range(chunks):
-        kv_copy(c, 0).start()
-        kv_copy(c, 1).start()
 
     barrier = pltpu.get_barrier_semaphore()
     pl.semaphore_signal(barrier, inc=1, device_id=sibling, device_id_type=MESH)
@@ -120,7 +96,6 @@
         pl.semaphore_signal(
             barrier, inc=1, device_id=device(lax.rem(hi + d, far), side, core), device_id_type=MESH
         )
-
     my_slot = slot_of(hi, side, core)
     qg[pl.ds(my_slot, 1)] = q_ref[...][None]
 
@@ -148,8 +123,33 @@
     gather_send(my_slot, across)
     gather_send(my_slot, sibling)
 
-    position = me * rows + lax.broadcasted_iota(jnp.int32, bias_row.shape, 1)
-    bias_row[...] = jnp.where(position < tok_ref[0], 0.0, NEG_FILL)
+    for d in range(1, far):
+        slot = slot_of(lax.rem(hi - d + far, far), side, core)
+        gather_wait(slot)
+        gather_send(slot, across)
+        gather_send(slot, sibling)
+    for d in range(far):
+        slot = slot_of(lax.rem(hi - d + far, far), 1 - side, core)
+        gather_wait(slot)
+        gather_send(slot, sibling)
+    for s_side in (side, 1 - side):
+        for d in range(far):
+            gather_wait(slot_of(lax.rem(hi - d + far, far), s_side, 1 - core))
+    for copy in sends:
+        copy.wait_send()
+
+
+def attend_kernel(n, heads, tok_ref, start_ref, q_ref, k_ref, v_ref, sk_ref, sv_ref, part, skp, svp):
+    rows = k_ref.shape[0]
+    own = sk_ref.shape[0]
+    chips = n // 2
+    far = chips // 2
+    total = n * own
+    cw = heads * HEAD_DIM
+    coef = math.log2(math.e) / math.sqrt(HEAD_DIM)
+    me = lax.axis_index("seq")
+    position = me * rows + lax.broadcasted_iota(jnp.int32, (1, rows), 1)
+    bias_row = jnp.where(position < tok_ref[0], 0.0, NEG_FILL)
     shape = (total, LANES)
     row = lax.broadcasted_iota(jnp.int32, shape, 0)
     lane = lax.broadcasted_iota(jnp.int32, shape, 1)
@@ -164,24 +164,80 @@
     for f in range(1, (FRAME_TOK - 1 + total) // FRAME_TOK + 1):
         edge = f * FRAME_TOK - start_ref[0]
         seen = jnp.logical_and(seen, jnp.logical_or(key < edge, token >= edge))
-    bias_span[...] = jnp.where(seen, 0.0, NEG_FILL)
-    pad = jnp.zeros((LANES - own, width), jnp.float32)
-    for ref, buf in ((sk_ref, kbuf), (sv_ref, vbuf)):
+    bias_span = jnp.where(seen, 0.0, NEG_FILL)
+    pad = jnp.zeros((LANES - own, cw), jnp.float32)
+    for ref, buf in ((sk_ref, skp), (sv_ref, svp)):
         block = jnp.concatenate([ref[...].astype(jnp.float32), pad], axis=0)
-        buf[pl.ds(rows, LANES), :] = block.astype(jnp.bfloat16)
-
+        buf[...] = block.astype(jnp.bfloat16)
+
+    def scores(j):
+        cut = slice(j * HEAD_DIM, (j + 1) * HEAD_DIM)
+        q = q_ref[:, :, cut].astype(jnp.float32).reshape(total, HEAD_DIM).astype(jnp.bfloat16)
+        nt = (((1,), (1,)), ((), ()))
+        s_cache = lax.dot_general(q, k_ref[:, cut], nt, preferred_element_type=jnp.float32)
+        s_span = lax.dot_general(q, skp[:, cut], nt, preferred_element_type=jnp.float32)
+        return s_cache * coef + bias_row, s_span * coef + bias_span
+
+    stats = jnp.zeros(shape, jnp.float32)
+    ahead = scores(0)
+    for j in range(heads):
+        s_cache, s_span = ahead
+        if j + 1 < heads:
+            ahead = scores(j + 1)
+        cut = slice(j * HEAD_DIM, (j + 1) * HEAD_DIM)
+        top = jnp.maximum(
+            jnp.max(s_cache, axis=1, keepdims=True), jnp.max(s_span, axis=1, keepdims=True)
+        )
+        high, low = two_parts(top)
+        top = high + low
+        w_cache, w_span = jnp.exp2(s_cache - top), jnp.exp2(s_span - top)
+        den = jnp.sum(w_cache, axis=1, keepdims=True) + jnp.sum(w_span, axis=1, keepdims=True)
+        num = jnp.dot(
+            w_cache.astype(jnp.bfloat16), v_ref[:, cut], preferred_element_type=jnp.float32
+        ) + jnp.dot(w_span.astype(jnp.bfloat16), svp[:, cut], preferred_element_type=jnp.float32)
+        part[0, :, :, cut] = num.reshape(n, own, HEAD_DIM)
+        stats = jnp.where(lane == j, top, stats)
+        stats = jnp.where(lane == 64 + j, den, stats)
+    part[0, :, :, cw:] = stats.reshape(n, own, LANES)
+
+
+def reduce_kernel(
+    n, part_ref, o_ref, part, ea, eb, ec, ra, rb, rc,
+    a_send, a_recv, b_send, b_recv, c_send, c_recv,
+):
+    chunks, _, own, cs = part_ref.shape
+    cw = cs - LANES
+    heads = cw // HEAD_DIM
+    chips = n // 2
+    far = chips // 2
+    me = lax.axis_index("seq")
+    group = lax.axis_index("groups")
+    core = lax.rem(me, 2)
+    side = lax.rem(me // 2, 2)
+    hi = me // 4
+
+    def device(hi_, side_, core_):
+        return (group, (hi_ * 2 + side_) * 2 + core_)
+
+    def slot_of(hi_, side_, core_):
+        return core_ * chips + side_ * far + hi_
+
+    sibling = device(hi, side, 1 - core)
+    across = device(hi, 1 - side, core)
+
+    barrier = pltpu.get_barrier_semaphore()
+    pl.semaphore_signal(barrier, inc=1, device_id=sibling, device_id_type=MESH)
+    pl.semaphore_signal(barrier, inc=1, device_id=across, device_id_type=MESH)
     for d in range(1, far):
-        slot = slot_of(lax.rem(hi - d + far, far), side, core)
-        gather_wait(slot)
-        gather_send(slot, across)
-        gather_send(slot, sibling)
-    for d in range(far):
-        slot = slot_of(lax.rem(hi - d + far, far), 1 - side, core)
-        gather_wait(slot)
-        gather_send(slot, sibling)
-    for s_side in (side, 1 - side):
-        for d in range(far):
-            gather_wait(slot_of(lax.rem(hi - d + far, far), s_side, 1 - core))
+        pl.semaphore_signal(
+            barrier, inc=1, device_id=device(lax.rem(hi + d, far), side, core), device_id_type=MESH
+        )
+
+    my_slot = slot_of(hi, side, core)
+    for c in range(chunks):
+        theirs = part_ref[c, pl.ds((1 - core) * chips, chips)]
+        ea[c] = code(theirs.reshape(chips * own, cs), heads)
+    pl.semaphore_wait(barrier, far + 1)
 
     def a_copy(c):
         return pltpu.make_async_remote_copy(
@@ -205,35 +261,10 @@
             device_id=device(other, side, core), device_id_type=MESH,
         )
 
-    def attend(c, first, last):
-        stat_lane = lax.broadcasted_iota(jnp.int32, (total, LANES), 1)
-        if first == 0:
-            stats = jnp.zeros((total, LANES), jnp.float32)
-        else:
-            stats = part[c, :, :, cw:].reshape(total, LANES)
-        for j in range(first, last):
-            cut = pl.ds(pl.multiple_of(c * cw + j * HEAD_DIM, LANES), HEAD_DIM)
-            q = qg[:, :, cut].astype(jnp.float32).reshape(total, HEAD_DIM).astype(jnp.bfloat16)
-            s = lax.dot_general(
-                q, kbuf[:, cut], (((1,), (1,)), ((), ())), preferred_element_type=jnp.float32
-            ) * coef
-            s_cache = s[:, :rows] + bias_row[...]
-            s_span = s[:, rows:] + bias_span[...]
-            s = jnp.concatenate([s_cache, s_span], axis=1)
-            high, low = two_parts(jnp.max(s, axis=1, keepdims=True))
-            top = high + low
-            w = jnp.exp2(s - top)
-            den = jnp.sum(w, axis=1, keepdims=True)
-            num = jnp.dot(w.astype(jnp.bfloat16), vbuf[:, cut], preferred_element_type=jnp.float32)
-            part[c, :, :, j * HEAD_DIM : (j + 1) * HEAD_DIM] = num.reshape(n, own, HEAD_DIM)
-            stats = jnp.where(stat_lane == j, top, stats)
-            stats = jnp.where(stat_lane == 64 + j, den, stats)
-        part[c, :, :, cw:] = stats.reshape(n, own, LANES)
-
     def merge_a(c):
         a_copy(c).wait_recv()
         mine = pl.ds(core * chips, chips)
-        x = part[c, mine].reshape(chips * own, cs)
+        x = part_ref[c, mine].reshape(chips * own, cs)
         x = merge(x, decode(ra[c], heads), heads)
         part[c, mine] = x.reshape(chips, own, cs)
         theirs = part[c, pl.ds(core * chips + (1 - side) * far, far)]
@@ -262,36 +293,21 @@
         cut = pl.ds(pl.multiple_of(c * cw, LANES), cw)
         o_ref[:, cut] = jnp.concatenate(out, axis=1).astype(jnp.bfloat16)
 
+    for c in range(chunks):
+        a_copy(c).start()
+
     def when(low, t, high, do, c):
         @pl.when(jnp.logical_and(t >= low, t < high))
         def _():
             do(c)
 
-    half = heads // 2
-
-    def open_chunk(c):
-        kv_copy(c, 0).wait()
-        kv_copy(c, 1).wait()
-        attend(c, 0, half)
-
-    def close_chunk(c):
-        attend(c, half, heads)
-        theirs = part[c, pl.ds((1 - core) * chips, chips)]
-        ea[c] = code(theirs.reshape(chips * own, cs), heads)
-        a_copy(c).start()
-
     def step(t, _):
-        when(0, t, chunks, open_chunk, t)
-        when(1, t, chunks + 1, merge_a, t - 1)
-        when(2, t, chunks + 2, merge_b, t - 2)
-        when(3, t, chunks + 3, finish, t - 3)
-        when(0, t, chunks, close_chunk, t)
+        when(0, t, chunks, merge_a, t)
+        when(1, t, chunks + 1, merge_b, t - 1)
+        when(2, t, chunks + 2, finish, t - 2)
         return 0
 
-    lax.fori_loop(0, chunks + 3, step, 0)
-
-    for copy in sends:
-        copy.wait_send()
+    lax.fori_loop(0, chunks + 2, step, 0)
     for c in range(chunks):
         a_copy(c).wait_send()
         b_copy(c).wait_send()
@@ -306,44 +322,54 @@
     chunks = 4 if heads % 4 == 0 else 1
     chips = n // 2
     far = chips // 2
-    total = n * own
-    cs = width // chunks + LANES
+    cw = width // chunks
+    cs = cw + LANES
     smem = pl.BlockSpec(memory_space=pltpu.SMEM)
     vmem = pl.BlockSpec(memory_space=pltpu.VMEM)
-    hbm = pl.BlockSpec(memory_space=pl.ANY)
     dma = pltpu.SemaphoreType.DMA
+    limit = 56 * 1024 * 1024
+    gathered = pl.pallas_call(
+        functools.partial(gather_kernel, n),
+        out_shape=jax.ShapeDtypeStruct((n, own, width), jnp.bfloat16),
+        in_specs=[vmem],
+        out_specs=vmem,
+        scratch_shapes=[dma((far - 1 + far + chips,)), dma((n,))],
+        compiler_params=pltpu.CompilerParams(
+            collective_id=0, has_side_effects=True, vmem_limit_bytes=limit
+        ),
+    )(queries)
+    part = pl.pallas_call(
+        functools.partial(attend_kernel, n, heads // chunks),
+        grid=(chunks,),
+        out_shape=jax.ShapeDtypeStruct((chunks, n, own, cs), jnp.float32),
+        in_specs=[
+            smem, smem,
+            pl.BlockSpec((n, own, cw), lambda i: (0, 0, i)),
+            pl.BlockSpec((rows, cw), lambda i: (0, i)),
+            pl.BlockSpec((rows, cw), lambda i: (0, i)),
+            pl.BlockSpec((own, cw), lambda i: (0, i)),
+            pl.BlockSpec((own, cw), lambda i: (0, i)),
+        ],
+        out_specs=pl.BlockSpec((1, n, own, cs), lambda i: (i, 0, 0, 0)),
+        scratch_shapes=[pltpu.VMEM((LANES, cw), jnp.bfloat16)] * 2,
+        compiler_params=pltpu.CompilerParams(vmem_limit_bytes=limit),
+    )(cache_tokens, span_start, gathered, cache_keys, cache_values, span_keys, span_values)
+    coded = [
+        pltpu.VMEM((chunks, chips * own, cs), jnp.bfloat16),
+        pltpu.VMEM((chunks, far * own, cs), jnp.bfloat16),
+        pltpu.VMEM((chunks, far - 1, own, cs), jnp.bfloat16),
+    ]
     return pl.pallas_call(
-        functools.partial(kernel, n, chunks),
+        functools.partial(reduce_kernel, n),
         out_shape=jax.ShapeDtypeStruct((own, width), jnp.bfloat16),
-        in_specs=[smem, smem, vmem, hbm, hbm, vmem, vmem],
+        in_specs=[vmem],
         out_specs=vmem,
-        scratch_shapes=[
-            pltpu.VMEM((n, own, width), jnp.bfloat16),
-            pltpu.VMEM((rows + LANES, width), jnp.bfloat16),
-            pltpu.VMEM((rows + LANES, width), jnp.bfloat16),
-            pltpu.VMEM((chunks, n, own, cs), jnp.float32),
-            pltpu.VMEM((chunks, chips * own, cs), jnp.bfloat16),
-            pltpu.VMEM((chunks, far * own, cs), jnp.bfloat16),
-            pltpu.VMEM((chunks, far - 1, own, cs), jnp.bfloat16),
-            pltpu.VMEM((chunks, chips * own, cs), jnp.bfloat16),
-            pltpu.VMEM((chunks, far * own, cs), jnp.bfloat16),
-            pltpu.VMEM((chunks, far - 1, own, cs), jnp.bfloat16),
-            pltpu.VMEM((1, rows), jnp.float32),
-            pltpu.VMEM((total, LANES), jnp.float32),
-            dma((2, chunks)),
-            dma((far - 1 + far + chips,)),
-            dma((n,)),
-            dma((chunks,)),
-            dma((chunks,)),
-            dma((chunks,)),
-            dma((chunks,)),
-            dma((chunks, far - 1)),
-            dma((chunks, far - 1)),
-        ],
+        scratch_shapes=[pltpu.VMEM((chunks, n, own, cs), jnp.float32)] + coded * 2
+        + [dma((chunks,))] * 4 + [dma((chunks, far - 1))] * 2,
         compiler_params=pltpu.CompilerParams(
-            collective_id=0, has_side_effects=True, vmem_limit_bytes=56 * 1024 * 1024
+            collective_id=1, has_side_effects=True, vmem_limit_bytes=limit
         ),
-    )(cache_tokens, span_start, queries, cache_keys, cache_values, span_keys, span_values)
+    )(part)
 
 
 def solution(mesh):

time: 42.7 us -> 50.8 us (1.19)
  Pallas kernels: 39.7 us -> 47.7 us
    pallas_call x1 -> x3, Pallas kernels: 39.7 us -> 47.7 us  [the longest x1 23 us: local(): pl.pallas_call(functools.partial(reduce_kernel, n), out_shape=jax.ShapeDt...]
where the time goes in v5:
time: 50.8 us; the launch traced here: 50.4 us
  Pallas kernels  47.7 us (94%)
  local copies, waits for them, and re-layouts  1.4 us (3%)
  between operations  1.31 us (3%)
    pallas_call x1, Pallas kernels, local(): pl.pallas_call(functools.partial(reduce_kernel, n), out_shape=jax.ShapeDt...  23 us
    pallas_call x1, Pallas kernels, local(): pl.pallas_call(functools.partial(gather_kernel, n), out_shape=jax.ShapeDt...  15.8 us
    pallas_call x1, Pallas kernels, local(): pl.pallas_call(functools.partial(attend_kernel, n, heads // chunks), grid...  8.84 us
    unnamed x1, local copies, waits for them, and re-layouts  1.4 us

profile of v5, /device:TPU:0, one launch (start us, length us, event | category | flops | bytes accessed | tf_op | source)
XLA Modules:
  0.0 50.4 jit_solution(13446673606331211125)
XLA Ops:
  1.3 15.8 %shard_map.73.q_ref = bf16[16,8,2560]{2,1,0:T(8,128)(2,1)} custom-call(bf16[8,2560]{1,0:T(8,128)(2,1)} %q_ref.1), custom_call_target="tpu_custom_call" | custom-call | tf_op jit(solution)/shard_map/pallas_call | solution.py:331
  17.1 8.8 %shard_map.74.part_ref = f32[4,16,8,768]{3,2,1,0:T(8,128)} custom-call(s32[1]{0:T(128)S(6)} %copy.9.tok_ref, s32[1]{0:T(128)S(6)} %copy.10.start_ref, bf16[16,8,2560]{2,1,0:T(8,128)(2,1)} %shard_map.73.q_ref, bf16[1024,2560]{1,0:T(8,128)(2,1)} %k_ref.1, bf16[1024,2560]{1,0:T(8,128)(2,1)} %v_ref.1, bf16[8,2560]{1,0:T(8,128)(2,1)} %sk_ref.1, ...), custom_call_target="tpu_custom_call" | custom-call | tf_op jit(solution)/shard_map/pallas_call | solution.py:341
  26.0 23.0 %shard_map.75 = bf16[8,2560]{1,0:T(8,128)(2,1)} custom-call(f32[4,16,8,768]{3,2,1,0:T(8,128)} %shard_map.74.part_ref), custom_call_target="tpu_custom_call" | custom-call | tf_op jit(solution)/shard_map/pallas_call | solution.py:362
  49.0 1.4 %copy.11 = bf16[8,2560]{1,0:T(8,128)(2,1)} copy(bf16[8,2560]{1,0:T(8,128)(2,1)} %shard_map.75) | data formatting | bytes 81920

commit v6 on v4

--- a/solution.py
+++ b/solution.py
@@ -79,6 +79,7 @@
 ):
     rows, width = k_hbm.shape
     own = q_ref.shape[0]
+    halves = qg.shape[0]
     chips = n // 2
     far = chips // 2
     total = n * own
@@ -122,31 +123,52 @@
         )
 
     my_slot = slot_of(hi, side, core)
-    qg[pl.ds(my_slot, 1)] = q_ref[...][None]
+    half_width = width // halves
+    for g in range(halves):
+        qg[g, pl.ds(my_slot, 1)] = q_ref[:, g * half_width : (g + 1) * half_width][None]
 
     pl.semaphore_wait(barrier, far + 1)
 
-    def gather_copy(slot, to, number):
+    def gather_copy(g, slot, to, number):
         return pltpu.make_async_remote_copy(
-            src_ref=qg.at[slot], dst_ref=qg.at[slot],
-            send_sem=g_send.at[number], recv_sem=g_recv.at[slot],
+            src_ref=qg.at[g, slot], dst_ref=qg.at[g, slot],
+            send_sem=g_send.at[g, number], recv_sem=g_recv.at[g, slot],
             device_id=to, device_id_type=MESH,
         )
 
-    sends = []
-
-    def gather_send(slot, to):
-        copy = gather_copy(slot, to, len(sends))
-        copy.start()
-        sends.append(copy)
-
-    def gather_wait(slot):
-        gather_copy(slot, sibling, 0).wait_recv()
-
-    for d in range(1, far):
-        gather_send(my_slot, device(lax.rem(hi + d, far), side, core))
-    gather_send(my_slot, across)
-    gather_send(my_slot, sibling)
+    def from_behind(d):
+        return lax.rem(hi - d + far, far)
+
+    def gather_wait(g, slot):
+        gather_copy(g, slot, sibling, 0).wait_recv()
+
+    def gather_own(g):
+        for d in range(1, far):
+            to = device(lax.rem(hi + d, far), side, core)
+            gather_copy(g, my_slot, to, d - 1).start()
+        gather_copy(g, my_slot, across, far - 1).start()
+        gather_copy(g, my_slot, sibling, 2 * far - 1).start()
+
+    def gather_far(g):
+        for d in range(1, far):
+            slot = slot_of(from_behind(d), side, core)
+            gather_wait(g, slot)
+            gather_copy(g, slot, across, far - 1 + d).start()
+            gather_copy(g, slot, sibling, 2 * far - 1 + d).start()
+
+    def gather_across(g):
+        for d in range(far):
+            slot = slot_of(from_behind(d), 1 - side, core)
+            gather_wait(g, slot)
+            gather_copy(g, slot, sibling, 3 * far - 1 + d).start()
+
+    def gather_sibling(g):
+        for s_side in (side, 1 - side):
+            for d in range(far):
+                gather_wait(g, slot_of(from_behind(d), s_side, 1 - core))
+
+    for g in range(halves):
+        gather_own(g)
 
     position = me * rows + lax.broadcasted_iota(jnp.int32, bias_row.shape, 1)
     bias_row[...] = jnp.where(position < tok_ref[0], 0.0, NEG_FILL)
@@ -170,18 +192,11 @@
         block = jnp.concatenate([ref[...].astype(jnp.float32), pad], axis=0)
         buf[pl.ds(rows, LANES), :] = block.astype(jnp.bfloat16)
 
-    for d in range(1, far):
-        slot = slot_of(lax.rem(hi - d + far, far), side, core)
-        gather_wait(slot)
-        gather_send(slot, across)
-        gather_send(slot, sibling)
-    for d in range(far):
-        slot = slot_of(lax.rem(hi - d + far, far), 1 - side, core)
-        gather_wait(slot)
-        gather_send(slot, sibling)
-    for s_side in (side, 1 - side):
-        for d in range(far):
-            gather_wait(slot_of(lax.rem(hi - d + far, far), s_side, 1 - core))
+    gather_far(0)
+    gather_across(0)
+    for g in range(1, halves):
+        gather_far(g)
+    gather_sibling(0)
 
     def a_copy(c):
         return pltpu.make_async_remote_copy(
@@ -211,15 +226,27 @@
             stats = jnp.zeros((total, LANES), jnp.float32)
         else:
             stats = part[c, :, :, cw:].reshape(total, LANES)
-        for j in range(first, last):
+        per = chunks // halves
+        base = lax.rem(c, per) * cw
+
+        def scores(j):
             cut = pl.ds(pl.multiple_of(c * cw + j * HEAD_DIM, LANES), HEAD_DIM)
-            q = qg[:, :, cut].astype(jnp.float32).reshape(total, HEAD_DIM).astype(jnp.bfloat16)
+            q_cut = pl.ds(pl.multiple_of(base + j * HEAD_DIM, LANES), HEAD_DIM)
+            q = qg[c // per, :, :, q_cut].astype(jnp.float32).reshape(total, HEAD_DIM)
             s = lax.dot_general(
-                q, kbuf[:, cut], (((1,), (1,)), ((), ())), preferred_element_type=jnp.float32
+                q.astype(jnp.bfloat16), kbuf[:, cut], (((1,), (1,)), ((), ())),
+                preferred_element_type=jnp.float32,
             ) * coef
             s_cache = s[:, :rows] + bias_row[...]
             s_span = s[:, rows:] + bias_span[...]
-            s = jnp.concatenate([s_cache, s_span], axis=1)
+            return jnp.concatenate([s_cache, s_span], axis=1)
+
+        ahead = scores(first)
+        for j in range(first, last):
+            s = ahead
+            if j + 1 < last:
+                ahead = scores(j + 1)
+            cut = pl.ds(pl.multiple_of(c * cw + j * HEAD_DIM, LANES), HEAD_DIM)
             high, low = two_parts(jnp.max(s, axis=1, keepdims=True))
             top = high + low
             w = jnp.exp2(s - top)
@@ -281,7 +308,11 @@
         a_copy(c).start()
 
     def step(t, _):
+        for g in range(1, halves):
+            when(g * (chunks // halves), t, g * (chunks // halves) + 1, gather_sibling, g)
         when(0, t, chunks, open_chunk, t)
+        for g in range(1, halves):
+            when(0, t, 1, gather_across, g)
         when(1, t, chunks + 1, merge_a, t - 1)
         when(2, t, chunks + 2, merge_b, t - 2)
         when(3, t, chunks + 3, finish, t - 3)
@@ -290,8 +321,9 @@
 
     lax.fori_loop(0, chunks + 3, step, 0)
 
-    for copy in sends:
-        copy.wait_send()
+    for g in range(halves):
+        for number in range(2 * far - 1 + chips):
+            gather_copy(g, my_slot, sibling, number).wait_send()
     for c in range(chunks):
         a_copy(c).wait_send()
         b_copy(c).wait_send()
@@ -304,6 +336,7 @@
     rows = cache_keys.shape[0]
     heads = width // HEAD_DIM
     chunks = 4 if heads % 4 == 0 else 1
+    halves = 2 if chunks % 2 == 0 else 1
     chips = n // 2
     far = chips // 2
     total = n * own
@@ -318,7 +351,7 @@
         in_specs=[smem, smem, vmem, hbm, hbm, vmem, vmem],
         out_specs=vmem,
         scratch_shapes=[
-            pltpu.VMEM((n, own, width), jnp.bfloat16),
+            pltpu.VMEM((halves, n, own, width // halves), jnp.bfloat16),
             pltpu.VMEM((rows + LANES, width), jnp.bfloat16),
             pltpu.VMEM((rows + LANES, width), jnp.bfloat16),
             pltpu.VMEM((chunks, n, own, cs), jnp.float32),
@@ -331,8 +364,8 @@
             pltpu.VMEM((1, rows), jnp.float32),
             pltpu.VMEM((total, LANES), jnp.float32),
             dma((2, chunks)),
-            dma((far - 1 + far + chips,)),
-            dma((n,)),
+            dma((halves, far - 1 + far + chips)),
+            dma((halves, n)),
             dma((chunks,)),
             dma((chunks,)),
             dma((chunks,)),

time: 42.7 us -> 41.3 us (0.967)
  Pallas kernels: 39.7 us -> 38.4 us
    pallas_call x1, Pallas kernels: 39.7 us -> 38.4 us  [local(): pl.pallas_call(functools.partial(kernel, n, chunks), out_shape=jax.ShapeD...]
where the time goes in v6:
time: 41.3 us; the launch traced here: 41.1 us
  Pallas kernels  38.4 us (93%)
  local copies, waits for them, and re-layouts  1.4 us (3%)
  between operations  1.3 us (3%)
    pallas_call x1, Pallas kernels, local(): pl.pallas_call(functools.partial(kernel, n, chunks), out_shape=jax.ShapeD...  38.4 us
    unnamed x1, local copies, waits for them, and re-layouts  1.4 us

profile of v6, /device:TPU:0, one launch (start us, length us, event | category | flops | bytes accessed | tf_op | source)
XLA Modules:
  0.0 41.1 jit_solution(16514930601168786700)
XLA Ops:
  1.3 38.4 %shard_map.73 = bf16[8,2560]{1,0:T(8,128)(2,1)} custom-call(s32[1]{0:T(128)S(6)} %copy.9.tok_ref, s32[1]{0:T(128)S(6)} %copy.10.start_ref, bf16[8,2560]{1,0:T(8,128)(2,1)} %q_ref.1, bf16[1024,2560]{1,0:T(8,128)(2,1)} %k_hbm.1, bf16[1024,2560]{1,0:T(8,128)(2,1)} %v_hbm.1, bf16[8,2560]{1,0:T(8,128)(2,1)} %sk_ref.1, bf16[8,2560]{1,0:T(8,128)(2,1)} %sv_ref.1), custom_call_target="tpu_custom_call" | custom-call | tf_op jit(solution)/shard_map/pallas_call | solution.py:348
  39.7 1.4 %copy.11 = bf16[8,2560]{1,0:T(8,128)(2,1)} copy(bf16[8,2560]{1,0:T(8,128)(2,1)} %shard_map.73) | data formatting | bytes 81920

commit v7 on v6

--- a/solution.py
+++ b/solution.py
@@ -74,8 +74,8 @@
 def kernel(
     n, chunks,
     tok_ref, start_ref, q_ref, k_hbm, v_hbm, sk_ref, sv_ref, o_ref,
-    qg, kbuf, vbuf, part, ea, eb, ec, ra, rb, rc, bias_row, bias_span,
-    kv_sem, g_send, g_recv, a_send, a_recv, b_send, b_recv, c_send, c_recv,
+    qg, kbuf, vbuf, part, ea, ec, ra, rc, bias_row, bias_span,
+    kv_sem, g_send, g_recv, a_send, a_recv, c_send, c_recv,
 ):
     rows, width = k_hbm.shape
     own = q_ref.shape[0]
@@ -102,6 +102,7 @@
 
     sibling = device(hi, side, 1 - core)
     across = device(hi, 1 - side, core)
+    partners = (sibling, across, device(hi, 1 - side, 1 - core))
 
     def kv_copy(c, which):
         cut = pl.ds(pl.multiple_of(c * cw, LANES), cw)
@@ -115,8 +116,8 @@
         kv_copy(c, 1).start()
 
     barrier = pltpu.get_barrier_semaphore()
-    pl.semaphore_signal(barrier, inc=1, device_id=sibling, device_id_type=MESH)
-    pl.semaphore_signal(barrier, inc=1, device_id=across, device_id_type=MESH)
+    for partner in partners:
+        pl.semaphore_signal(barrier, inc=1, device_id=partner, device_id_type=MESH)
     for d in range(1, far):
         pl.semaphore_signal(
             barrier, inc=1, device_id=device(lax.rem(hi + d, far), side, core), device_id_type=MESH
@@ -127,7 +128,7 @@
     for g in range(halves):
         qg[g, pl.ds(my_slot, 1)] = q_ref[:, g * half_width : (g + 1) * half_width][None]
 
-    pl.semaphore_wait(barrier, far + 1)
+    pl.semaphore_wait(barrier, far + 2)
 
     def gather_copy(g, slot, to, number):
         return pltpu.make_async_remote_copy(
@@ -198,18 +199,11 @@
         gather_far(g)
     gather_sibling(0)
 
-    def a_copy(c):
+    def a_copy(c, k):
         return pltpu.make_async_remote_copy(
-            src_ref=ea.at[c], dst_ref=ra.at[c],
-            send_sem=a_send.at[c], recv_sem=a_recv.at[c],
-            device_id=sibling, device_id_type=MESH,
-        )
-
-    def b_copy(c):
-        return pltpu.make_async_remote_copy(
-            src_ref=eb.at[c], dst_ref=rb.at[c],
-            send_sem=b_send.at[c], recv_sem=b_recv.at[c],
-            device_id=across, device_id_type=MESH,
+            src_ref=ea.at[c, k], dst_ref=ra.at[c, k],
+            send_sem=a_send.at[c, k], recv_sem=a_recv.at[c, k],
+            device_id=partners[k], device_id_type=MESH,
         )
 
     def c_copy(c, d):
@@ -257,21 +251,17 @@
             stats = jnp.where(stat_lane == 64 + j, den, stats)
         part[c, :, :, cw:] = stats.reshape(n, own, LANES)
 
-    def merge_a(c):
-        a_copy(c).wait_recv()
-        mine = pl.ds(core * chips, chips)
-        x = part[c, mine].reshape(chips * own, cs)
-        x = merge(x, decode(ra[c], heads), heads)
-        part[c, mine] = x.reshape(chips, own, cs)
-        theirs = part[c, pl.ds(core * chips + (1 - side) * far, far)]
-        eb[c] = code(theirs.reshape(far * own, cs), heads)
-        b_copy(c).start()
-
-    def merge_b(c):
-        b_copy(c).wait_recv()
+    def merge_near(c):
+        for k in range(3):
+            a_copy(c, k).wait_recv()
         mine = pl.ds(core * chips + side * far, far)
         x = part[c, mine].reshape(far * own, cs)
-        x = merge(x, decode(rb[c], heads), heads)
+        y = decode(ra[c].reshape(3 * far * own, cs), heads)
+        cuts = [y[k * far * own : (k + 1) * far * own] for k in range(3)]
+        pairs = merge(
+            jnp.concatenate([x, cuts[0]], axis=0), jnp.concatenate([cuts[1], cuts[2]], axis=0), heads
+        )
+        x = merge(pairs[: far * own], pairs[far * own :], heads)
         part[c, mine] = x.reshape(far, own, cs)
         for d in range(1, far):
             ec[c, d - 1] = code(part[c, slot_of(lax.rem(hi + d, far), side, core)], heads)
@@ -303,9 +293,11 @@
 
     def close_chunk(c):
         attend(c, half, heads)
-        theirs = part[c, pl.ds((1 - core) * chips, chips)]
-        ea[c] = code(theirs.reshape(chips * own, cs), heads)
-        a_copy(c).start()
+        places = ((side, 1 - core), (1 - side, core), (1 - side, 1 - core))
+        for k, (side_, core_) in enumerate(places):
+            theirs = part[c, pl.ds(core_ * chips + side_ * far, far)]
+            ea[c, k] = code(theirs.reshape(far * own, cs), heads)
+            a_copy(c, k).start()
 
     def step(t, _):
         for g in range(1, halves):
@@ -313,20 +305,19 @@
         when(0, t, chunks, open_chunk, t)
         for g in range(1, halves):
             when(0, t, 1, gather_across, g)
-        when(1, t, chunks + 1, merge_a, t - 1)
-        when(2, t, chunks + 2, merge_b, t - 2)
-        when(3, t, chunks + 3, finish, t - 3)
         when(0, t, chunks, close_chunk, t)
+        when(1, t, chunks + 1, merge_near, t - 1)
+        when(2, t, chunks + 2, finish, t - 2)
         return 0
 
-    lax.fori_loop(0, chunks + 3, step, 0)
+    lax.fori_loop(0, chunks + 2, step, 0)
 
     for g in range(halves):
         for number in range(2 * far - 1 + chips):
             gather_copy(g, my_slot, sibling, number).wait_send()
     for c in range(chunks):
-        a_copy(c).wait_send()
-        b_copy(c).wait_send()
+        for k in range(3):
+            a_copy(c, k).wait_send()
         for d in range(1, far):
             c_copy(c, d).wait_send()
 
@@ -355,21 +346,17 @@
             pltpu.VMEM((rows + LANES, width), jnp.bfloat16),
             pltpu.VMEM((rows + LANES, width), jnp.bfloat16),
             pltpu.VMEM((chunks, n, own, cs), jnp.float32),
-            pltpu.VMEM((chunks, chips * own, cs), jnp.bfloat16),
-            pltpu.VMEM((chunks, far * own, cs), jnp.bfloat16),
+            pltpu.VMEM((chunks, 3, far * own, cs), jnp.bfloat16),
             pltpu.VMEM((chunks, far - 1, own, cs), jnp.bfloat16),
-            pltpu.VMEM((chunks, chips * own, cs), jnp.bfloat16),
-            pltpu.VMEM((chunks, far * own, cs), jnp.bfloat16),
+            pltpu.VMEM((chunks, 3, far * own, cs), jnp.bfloat16),
             pltpu.VMEM((chunks, far - 1, own, cs), jnp.bfloat16),
             pltpu.VMEM((1, rows), jnp.float32),
             pltpu.VMEM((total, LANES), jnp.float32),
             dma((2, chunks)),
             dma((halves, far - 1 + far + chips)),
             dma((halves, n)),
-            dma((chunks,)),
-            dma((chunks,)),
-            dma((chunks,)),
-            dma((chunks,)),
+            dma((chunks, 3)),
+            dma((chunks, 3)),
             dma((chunks, far - 1)),
             dma((chunks, far - 1)),
         ],

time: 41.3 us -> 40 us (0.969)
  Pallas kernels: 38.4 us -> 37.1 us
    pallas_call x1, Pallas kernels: 38.4 us -> 37.1 us  [local(): pl.pallas_call(functools.partial(kernel, n, chunks), out_shape=jax.ShapeD...]
where the time goes in v7:
time: 40 us; the launch traced here: 39.8 us
  Pallas kernels  37.1 us (93%)
  local copies, waits for them, and re-layouts  1.4 us (4%)
  between operations  1.3 us (3%)
    pallas_call x1, Pallas kernels, local(): pl.pallas_call(functools.partial(kernel, n, chunks), out_shape=jax.ShapeD...  37.1 us
    unnamed x1, local copies, waits for them, and re-layouts  1.4 us

profile of v7, /device:TPU:0, one launch (start us, length us, event | category | flops | bytes accessed | tf_op | source)
XLA Modules:
  0.0 39.8 jit_solution(2545177863278897733)
XLA Ops:
  1.3 37.1 %shard_map.73 = bf16[8,2560]{1,0:T(8,128)(2,1)} custom-call(s32[1]{0:T(128)S(6)} %copy.9.tok_ref, s32[1]{0:T(128)S(6)} %copy.10.start_ref, bf16[8,2560]{1,0:T(8,128)(2,1)} %q_ref.1, bf16[1024,2560]{1,0:T(8,128)(2,1)} %k_hbm.1, bf16[1024,2560]{1,0:T(8,128)(2,1)} %v_hbm.1, bf16[8,2560]{1,0:T(8,128)(2,1)} %sk_ref.1, bf16[8,2560]{1,0:T(8,128)(2,1)} %sv_ref.1), custom_call_target="tpu_custom_call" | custom-call | tf_op jit(solution)/shard_map/pallas_call | solution.py:339
  38.4 1.4 %copy.11 = bf16[8,2560]{1,0:T(8,128)(2,1)} copy(bf16[8,2560]{1,0:T(8,128)(2,1)} %shard_map.73) | data formatting | bytes 81920

commit v8 on v7

--- a/solution.py
+++ b/solution.py
@@ -209,7 +209,7 @@
     def c_copy(c, d):
         other = lax.rem(hi + d, far)
         return pltpu.make_async_remote_copy(
-            src_ref=ec.at[c, d - 1], dst_ref=rc.at[c, d - 1],
+            src_ref=ec.at[c, other], dst_ref=rc.at[c, d - 1],
             send_sem=c_send.at[c, d - 1], recv_sem=c_recv.at[c, d - 1],
             device_id=device(other, side, core), device_id_type=MESH,
         )
@@ -263,15 +263,17 @@
         )
         x = merge(pairs[: far * own], pairs[far * own :], heads)
         part[c, mine] = x.reshape(far, own, cs)
-        for d in range(1, far):
-            ec[c, d - 1] = code(part[c, slot_of(lax.rem(hi + d, far), side, core)], heads)
+        ec[c] = code(x, heads).reshape(far, own, cs)
+        for d in range(1, far):
             c_copy(c, d).start()
 
     def finish(c):
         x = part[c, my_slot]
         for d in range(1, far):
             c_copy(c, d).wait_recv()
-            x = merge(x, decode(rc[c, d - 1], heads), heads)
+        y = decode(rc[c].reshape((far - 1) * own, cs), heads)
+        for d in range(1, far):
+            x = merge(x, y[(d - 1) * own : d * own], heads)
         out = [
             x[:, j * HEAD_DIM : (j + 1) * HEAD_DIM] / x[:, cw + 64 + j : cw + 65 + j]
             for j in range(heads)
@@ -347,7 +349,7 @@
             pltpu.VMEM((rows + LANES, width), jnp.bfloat16),
             pltpu.VMEM((chunks, n, own, cs), jnp.float32),
             pltpu.VMEM((chunks, 3, far * own, cs), jnp.bfloat16),
-            pltpu.VMEM((chunks, far - 1, own, cs), jnp.bfloat16),
+            pltpu.VMEM((chunks, far, own, cs), jnp.bfloat16),
             pltpu.VMEM((chunks, 3, far * own, cs), jnp.bfloat16),
             pltpu.VMEM((chunks, far - 1, own, cs), jnp.bfloat16),
             pltpu.VMEM((1, rows), jnp.float32),

time: 40 us -> 40 us (level)
  no operation moved by 1% of the time
where the time goes in v8:
time: 40 us; the launch traced here: 39.7 us
  Pallas kernels  37 us (92%)
  local copies, waits for them, and re-layouts  1.4 us (4%)
  between operations  1.3 us (3%)
    pallas_call x1, Pallas kernels, local(): pl.pallas_call(functools.partial(kernel, n, chunks), out_shape=jax.ShapeD...  37 us
    unnamed x1, local copies, waits for them, and re-layouts  1.4 us

profile of v8, /device:TPU:0, one launch (start us, length us, event | category | flops | bytes accessed | tf_op | source)
XLA Modules:
  0.0 39.7 jit_solution(14875360339125038389)
XLA Ops:
  1.3 37.0 %shard_map.73 = bf16[8,2560]{1,0:T(8,128)(2,1)} custom-call(s32[1]{0:T(128)S(6)} %copy.9.tok_ref, s32[1]{0:T(128)S(6)} %copy.10.start_ref, bf16[8,2560]{1,0:T(8,128)(2,1)} %q_ref.1, bf16[1024,2560]{1,0:T(8,128)(2,1)} %k_hbm.1, bf16[1024,2560]{1,0:T(8,128)(2,1)} %v_hbm.1, bf16[8,2560]{1,0:T(8,128)(2,1)} %sk_ref.1, bf16[8,2560]{1,0:T(8,128)(2,1)} %sv_ref.1), custom_call_target="tpu_custom_call" | custom-call | tf_op jit(solution)/shard_map/pallas_call | solution.py:341
  38.3 1.4 %copy.11 = bf16[8,2560]{1,0:T(8,128)(2,1)} copy(bf16[8,2560]{1,0:T(8,128)(2,1)} %shard_map.73) | data formatting | bytes 81920
